TPU v7x, 256 devices: a whole 4x4x8 slice. The times are simulated.
256 devices in a mesh: blk: 64 (over y_lo, x, z), rep: 4 (over y_hi, core).
Axes of the slice: x: 4, y: 4 (y_hi: 2, y_lo: 2; y = y_hi * 2 + y_lo), z: 8, core: 2. Of those that a mesh axis runs over, the one named last changes fastest.
Arguments:
- node_features: bfloat16 [512, 65536], P('rep', 'blk'), may hold values from -6 to 6
- weight_first: bfloat16 [512, 512], P('rep'), may hold values from -0.25 to 0.25
- weight_second: bfloat16 [512, 512], P('rep'), may hold values from -0.25 to 0.25
- tiles: bfloat16 [256, 6, 256, 256], P('blk'), may hold values from -0.375 to 0.375
- slot_blocks: int32 [256, 6], P('blk'), may hold values from 0 to 255, as said below
- degrees: int32 [256], P('blk'), may hold values from 1 to 6, as said below
- block_position: int32 [256], replicated, may hold values from 0 to 255, as said below
- cotangent: bfloat16 [512, 65536], P('rep', 'blk'), may hold values from -6 to 6
Outputs:
- layer_output: bfloat16 [512, 65536], P('rep', 'blk')
- grad_first: float32 [512, 512], P('rep')
- grad_second: float32 [512, 512], P('rep')
Inputs may be any that keep to these rules, and one draw needn't show every extreme that they name: block_position[slot_blocks[b, 0]] = b. For every slot, block_position[slot_blocks[b, t]] // 4 differs from b // 4 by at most 2 modulo 256 // 4. Slots t >= degrees[b] are unused; the value 6 occurs. `block_position`: A permutation of 0 to 255.
All inputs are finite; a program needn't handle non-finite values.
Results may differ from a plain program's by a relative error of at most 0.025.
Values may be sent and summed in bfloat16 or wider, within the bound.
No kernel may reach another device: no remote copies, remote signals or barrier semaphores. Data moves between devices by JAX's collectives and lax.ppermute only.
A program may use at most 64 MiB of HBM per device.

v0:
```python
import jax
import jax.numpy as jnp
from jax import lax
from jax.sharding import PartitionSpec as P


def from_behind(array, axis, by):
    peers = lax.axis_size(axis)
    return lax.ppermute(array, axis, [(i, (i + by) % peers) for i in range(peers)])


def silu_slope(value):
    sigma = jax.nn.sigmoid(value)
    return sigma * (1.0 + value * (1.0 - sigma))


def body(
    node_features,
    weight_first,
    weight_second,
    tiles,
    slot_blocks,
    degrees,
    block_position,
    cotangent,
):
    width = node_features.shape[0]
    blocks = tiles.shape[0]
    slot_count = tiles.shape[1]
    block = tiles.shape[2]
    node_local = blocks * block
    axis_count = lax.axis_size("blk")
    reach = max(1, axis_count // 32)
    here = lax.axis_index("blk")
    node_count = node_local * axis_count
    total_blocks = blocks * axis_count
    matches = slot_blocks[:, :, None] == jnp.arange(total_blocks, dtype=jnp.int32)[None, None, :]
    position = jnp.sum(jnp.where(matches, block_position[None, None, :], 0), axis=2)
    owner = position // blocks
    inner = (position % blocks).reshape(-1)
    live = jnp.arange(slot_count, dtype=jnp.int32)[None, :] < degrees[:, None]
    offset_key = jnp.where(live, (owner - here + reach) % axis_count, 2 * reach + 1).reshape(-1)
    order = jnp.argsort(offset_key, stable=True)
    counts = jnp.sum(
        (offset_key[None, :] == jnp.arange(2 * reach + 2, dtype=jnp.int32)[:, None]).astype(
            jnp.int32
        ),
        axis=1,
    )
    starts = jnp.cumsum(counts) - counts
    scales = lax.rsqrt(degrees.astype(jnp.float32))
    empty = jnp.zeros((width, blocks, block), jnp.float32)

    def forward_add(total, held, key_value):
        held_blocks = held.reshape(width, blocks, block)

        def forward_one_slot(place, carry):
            slot = order[place]
            row = slot // slot_count
            column = slot % slot_count
            source = lax.dynamic_index_in_dim(held_blocks, inner[slot], 1, keepdims=False)
            part = lax.dot_general(
                source,
                tiles[row, column],
                (((1,), (1,)), ((), ())),
                preferred_element_type=jnp.float32,
            )
            return carry.at[:, row].add(part)

        first_place = starts[key_value]
        return lax.fori_loop(first_place, first_place + counts[key_value], forward_one_slot, total)

    def aggregate(values):
        held = from_behind(values, "blk", -reach)

        def aggregate_advance(step, carry):
            held, total = carry
            moved = from_behind(held, "blk", 1)
            total = forward_add(total, held, 2 * reach - step)
            return (moved, total)

        held, total = lax.fori_loop(0, 2 * reach, aggregate_advance, (held, empty))
        total = forward_add(total, held, 0)
        return (total * scales[None, :, None]).reshape(width, node_local)

    def mix(weights, features):
        return lax.psum_scatter(
            lax.dot_general(
                weights, features, (((0,), (0,)), ((), ())), preferred_element_type=jnp.float32
            ).astype(jnp.bfloat16),
            "rep",
            scatter_dimension=0,
            tiled=True,
        ).astype(jnp.float32)

    ax_rows = aggregate(node_features).astype(jnp.bfloat16)
    first = mix(weight_first, ax_rows)
    hidden = jax.nn.silu(first).astype(jnp.bfloat16)
    ah_rows = aggregate(hidden).astype(jnp.bfloat16)
    layer_output = mix(weight_second, ah_rows).astype(jnp.bfloat16)
    piece = lax.all_gather(cotangent, "rep", axis=0, tiled=True)
    back_sum = jnp.dot(weight_second, piece, preferred_element_type=jnp.float32)
    product = lax.dot_general(
        ah_rows, piece, (((1,), (1,)), ((), ())), preferred_element_type=jnp.float32
    )
    outer = product
    back_sum, outer = (back_sum, outer)
    factor = node_count ** (-0.5)
    summed_second = lax.psum(outer, "blk")
    back = back_sum.astype(jnp.bfloat16)
    gradient_blocks = back.reshape(width, blocks, block)

    def transpose_add(total, key_value):

        def transpose_one_slot(place, carry):
            slot = order[place]
            row = slot // slot_count
            column = slot % slot_count
            source = lax.dynamic_index_in_dim(gradient_blocks, row, 1, keepdims=False)
            part = (
                jnp.dot(source, tiles[row, column], preferred_element_type=jnp.float32)
                * scales[row]
            )
            return carry.at[:, inner[slot]].add(part)

        first_place = starts[key_value]
        return lax.fori_loop(
            first_place, first_place + counts[key_value], transpose_one_slot, total
        )

    total = transpose_add(empty, 0)

    def spread_advance(step, total):
        total = from_behind(total.astype(jnp.bfloat16), "blk", -1).astype(total.dtype)
        return transpose_add(total, step + 1)

    total = lax.fori_loop(0, 2 * reach, spread_advance, total)
    total = from_behind(total.astype(jnp.bfloat16), "blk", reach).astype(total.dtype)
    spread_rows = total.reshape(width, node_local)
    hidden_grad = (spread_rows * silu_slope(first)).astype(jnp.bfloat16)
    first_term = lax.dot_general(
        ax_rows,
        lax.all_gather(hidden_grad, "rep", axis=0, tiled=True),
        (((1,), (1,)), ((), ())),
        preferred_element_type=jnp.float32,
    )
    summed_first = lax.psum(first_term, "blk")
    return (layer_output, summed_first * factor, summed_second * factor)


def solution(mesh):
    return jax.shard_map(
        body,
        mesh=mesh,
        in_specs=(
            P("rep", "blk"),
            P("rep", None),
            P("rep", None),
            P("blk", None, None, None),
            P("blk", None),
            P("blk"),
            P(),
            P("rep", "blk"),
        ),
        out_specs=(P("rep", "blk"), P("rep", None), P("rep", None)),
        check_vma=False,
    )
```

profile of v0, /device:TPU:8, one launch (start us, length us, event | category | flops | bytes accessed | tf_op | source)
XLA Modules:
  0.0 1365.6 jit_solution(4118456267144331380)
XLA Ops:
  8.4 8.5 collective-permute-start.3
  24.7 3.3 collective-permute-done.3
  28.1 157.1 %while.170 = (s32[]{:T(128)}, bf16[128,1024]{0,1:T(8,128)(2,1)S(1)}, f32[128,4,256]{2,0,1:T(8,128)S(1)}, s32[6]{0:T(128)}, s32[6]{0:T(128)S(1)}, /*index=5*/s32[...) while((s32[]{:T(128)}, bf16[128,1024]{0,1:T(8,128)(2,1)S(1)}, ...), condition=%wide.region_8.9_spmd, body=%wide.region_4.8_spmd.sunk | while | flops 16842804 | bytes 2034054 | solution.py:82
  31.9 26.8 %while.178 = (s32[]{:T(128)}, f32[128,4,256]{2,0,1:T(8,128)S(1)}, s32[]{:T(128)}, s32[24]{0:T(128)S(1)}, s32[24]{0:T(128)S(1)}, /*index=5*/bf16[128,4,256]{0,2,1...) while((s32[]{:T(128)}, f32[128,4,256]{2,0,1:T(8,128)S(1)}, ...), condition=%wide.region_7.7_spmd, body=%wide.region_5.6_spmd.sunk | while | flops 16842796 | bytes 460767 | solution.py:71
  63.1 8.4 collective-permute-done.2
  75.2 92.5 %while.178 = (s32[]{:T(128)}, f32[128,4,256]{2,0,1:T(8,128)S(1)}, s32[]{:T(128)}, s32[24]{0:T(128)S(1)}, s32[24]{0:T(128)S(1)}, /*index=5*/bf16[128,4,256]{0,2,1...) while((s32[]{:T(128)}, f32[128,4,256]{2,0,1:T(8,128)S(1)}, ...), condition=%wide.region_7.7_spmd, body=%wide.region_5.6_spmd.sunk | while | flops 16842796 | bytes 460767 | solution.py:71
  171.5 13.7 %while.178 = (s32[]{:T(128)}, f32[128,4,256]{2,0,1:T(8,128)S(1)}, s32[]{:T(128)}, s32[24]{0:T(128)S(1)}, s32[24]{0:T(128)S(1)}, /*index=5*/bf16[128,4,256]{0,2,1...) while((s32[]{:T(128)}, f32[128,4,256]{2,0,1:T(8,128)S(1)}, ...), condition=%wide.region_7.7_spmd, body=%wide.region_5.6_spmd.sunk | while | flops 16842796 | bytes 460767 | solution.py:71
  185.2 10.5 while.171
  194.0 1.8 fusion.94
  199.6 10.6 while.175
  208.0 2.3 fusion.100
  210.2 174.0 %while.177 = (s32[]{:T(128)}, f32[128,4,256]{2,0,1:T(8,128)S(1)}, s32[6]{0:T(128)}, s32[6]{0:T(128)S(1)}, s32[24]{0:T(128)S(1)}, /*index=5*/s32[24]{0:T(128)S(1)...) while((s32[]{:T(128)}, f32[128,4,256]{2,0,1:T(8,128)S(1)}, ...), condition=%wide.region_29.30_spmd, body=%wide.region_25.29_spmd.sunk | while | flops 17137712 | bytes 3084182 | solution.py:137
  213.5 3.5 collective-permute-done
  217.1 15.0 %while.180 = (s32[]{:T(128)}, f32[128,4,256]{2,0,1:T(8,128)S(1)}, s32[]{:T(128)}, s32[24]{0:T(128)S(1)}, s32[24]{0:T(128)S(1)}, /*index=5*/bf16[128,4,256]{2,0,1...) while((s32[]{:T(128)}, f32[128,4,256]{2,0,1:T(8,128)S(1)}, ...), condition=%wide.region_28.28_spmd, body=%wide.region_26.27_spmd.sunk | while | flops 16875564 | bytes 462315 | solution.py:127
  227.8 2.4 fusion.103
  235.3 3.2 collective-permute-done
  238.6 100.9 %while.180 = (s32[]{:T(128)}, f32[128,4,256]{2,0,1:T(8,128)S(1)}, s32[]{:T(128)}, s32[24]{0:T(128)S(1)}, s32[24]{0:T(128)S(1)}, /*index=5*/bf16[128,4,256]{2,0,1...) while((s32[]{:T(128)}, f32[128,4,256]{2,0,1:T(8,128)S(1)}, ...), condition=%wide.region_28.28_spmd, body=%wide.region_26.27_spmd.sunk | while | flops 16875564 | bytes 462315 | solution.py:127
  249.3 2.4 fusion.103
  263.6 2.4 fusion.103
  278.0 2.4 fusion.103
  292.3 2.4 fusion.103
  306.6 2.4 fusion.103
  320.9 2.4 fusion.103
  335.2 2.4 fusion.103
  342.7 4.5 collective-permute-done
  348.0 3.0 collective-permute-start
  355.0 29.3 %while.180 = (s32[]{:T(128)}, f32[128,4,256]{2,0,1:T(8,128)S(1)}, s32[]{:T(128)}, s32[24]{0:T(128)S(1)}, s32[24]{0:T(128)S(1)}, /*index=5*/bf16[128,4,256]{2,0,1...) while((s32[]{:T(128)}, f32[128,4,256]{2,0,1:T(8,128)S(1)}, ...), condition=%wide.region_28.28_spmd, body=%wide.region_26.27_spmd.sunk | while | flops 16875564 | bytes 462315 | solution.py:127
  365.7 2.4 fusion.103
  380.0 2.4 fusion.103
  384.3 4.0 collective-permute-start.5
  388.2 7.6 collective-permute-done.5
  398.2 18.3 %collective-permute-done.4 = bf16[128,1024]{0,1:T(8,128)(2,1)S(1)} collective-permute-done((bf16[128,1024]{0,1:T(8,128)(2,1)S(1)}, bf16[128,1024]{0,1:T(8,128)(2,1)S(1)}, u32[]{:S(2)}, u32[]{:S(2)}) %collective-permute-start.4) | collective-permute-done | bytes 262176 | tf_op jit(solution)/shard_map/ppermute | solution.py:9
  416.6 154.4 %while.173 = (s32[]{:T(128)}, bf16[128,1024]{0,1:T(8,128)(2,1)S(1)}, f32[128,4,256]{2,0,1:T(8,128)S(1)}, s32[6]{0:T(128)}, s32[6]{0:T(128)S(1)}, /*index=5*/s32[...) while((s32[]{:T(128)}, bf16[128,1024]{0,1:T(8,128)(2,1)S(1)}, ...), condition=%wide.region_17.18_spmd, body=%wide.region_13.17_spmd.sunk | while | flops 16842804 | bytes 2034054 | solution.py:82
  420.4 26.5 %while.179 = (s32[]{:T(128)}, f32[128,4,256]{2,0,1:T(8,128)S(1)}, s32[]{:T(128)}, s32[24]{0:T(128)S(1)}, s32[24]{0:T(128)S(1)}, /*index=5*/bf16[128,4,256]{0,2,1...) while((s32[]{:T(128)}, f32[128,4,256]{2,0,1:T(8,128)S(1)}, ...), condition=%wide.region_16.16_spmd, body=%wide.region_14.15_spmd.sunk | while | flops 16842796 | bytes 460767 | solution.py:71
  430.4 1.8 fusion.106
  443.4 1.8 fusion.106
  451.4 7.1 collective-permute-done.1
  462.3 91.3 %while.179 = (s32[]{:T(128)}, f32[128,4,256]{2,0,1:T(8,128)S(1)}, s32[]{:T(128)}, s32[24]{0:T(128)S(1)}, s32[24]{0:T(128)S(1)}, /*index=5*/bf16[128,4,256]{0,2,1...) while((s32[]{:T(128)}, f32[128,4,256]{2,0,1:T(8,128)S(1)}, ...), condition=%wide.region_16.16_spmd, body=%wide.region_14.15_spmd.sunk | while | flops 16842796 | bytes 460767 | solution.py:71
  472.3 1.8 fusion.106
  485.3 1.8 fusion.106
  498.2 1.8 fusion.106
  524.2 1.8 fusion.106
  557.4 13.6 while.179
  571.0 13.9 %while.174 = (s32[]{:T(128)}, f32[128,4,256]{2,0,1:T(8,128)S(1)}, s32[]{:T(128)}, s32[24]{0:T(128)S(1)}, s32[24]{0:T(128)S(1)}, /*index=5*/bf16[128,4,256]{0,2,1...) while((s32[]{:T(128)}, f32[128,4,256]{2,0,1:T(8,128)S(1)}, ...), condition=%wide.region_20.21_spmd, body=%wide.region_18.20_spmd.sunk | while | flops 16842796 | bytes 460767 | solution.py:71
  586.5 2.3 fusion.62
  590.6 731.1 %all-reduce.3.cloned.1.call-done = (f32[128,512]{1,0:T(8,128)}, f32[128,512]{1,0:T(8,128)}) async-done(((f32[128,512]{1,0:T(8,128)}, f32[128,512]{1,0:T(8,128)}), (f32[128,512]{1,0:T(8,128)}, f32[128,512]{1,0:T(8,128)})) %all-reduce.3.cloned.1.call-update) | async-done | bytes 524304 | tf_op jit(solution)/shard_map/psum | solution.py:147
  1321.7 1.9 broadcast_multiply_fusion
  1323.6 35.6 %reduce-scatter.9.cloned.1.call-done = bf16[128,1024]{1,0:T(8,128)(2,1)} async-done(((bf16[512,1024]{1,0:T(8,128)(2,1)}), bf16[128,1024]{1,0:T(8,128)(2,1)}) %reduce-scatter.9.cloned.1.call-update) | async-done | bytes 262160
  (240 shorter events, 153.0 us)
Async XLA Ops:
  7.2 190.8 %copy-start = (bf16[128,512]{1,0:T(8,128)(2,1)S(1)}, bf16[128,512]{1,0:T(8,128)(2,1)}, u32[]{:S(2)}) copy-start(bf16[128,512]{1,0:T(8,128)(2,1)} %param.40) | copy-start | bytes 393220
  7.2 190.8 %all-gather.3.cloned.1.call-start = ((), (), s32[]{:S(2)}) async-start(), calls=%async_computation.2 | async-start | bytes 1310720 | tf_op jit(solution)/shard_map/all_gather | solution.py:101
  8.4 19.6 %collective-permute-start.3 = (bf16[128,1024]{0,1:T(8,128)(2,1)S(1)}, bf16[128,1024]{0,1:T(8,128)(2,1)S(1)}, u32[]{:S(2)}, u32[]{:S(2)}) collective-permute-start(bf16[128,1024]{0,1:T(8,128)(2,1)S(1)} %copy.47), channel_id=1, source_target_pairs={{0,248},{4,252},{8,0},{12,4},{16,8},{20,12},{24,16},{28,20},{32,24... | collective-permute-start | bytes 786440 | tf_op jit(solution)/shard_map/ppermute | solution.py:9
  16.9 379.2 %reduce-scatter.7.cloned.1.call-start = ((), (), s32[]{:S(2)}) async-start(), calls=%async_computation.4 | async-start | bytes 1310720
  28.8 29.9 %collective-permute-start.2 = (bf16[128,1024]{0,1:T(8,128)(2,1)}, bf16[128,1024]{0,1:T(8,128)(2,1)S(1)}, u32[]{:S(2)}, u32[]{:S(2)}) collective-permute-start(bf16[128,1024]{0,1:T(8,128)(2,1)} %copy.95), channel_id=1, source_target_pairs={{0,4},{4,8},{8,12},{12,16},{16,20},{20,24},{24,28},{28,32},{32,36}... | collective-permute-start | bytes 786440 | tf_op jit(solution)/shard_map/while/body/eval_jaxpr/ppermute | solution.py:9
  59.4 12.0 collective-permute-start.2
  72.1 95.6 %collective-permute-start.2 = (bf16[128,1024]{0,1:T(8,128)(2,1)}, bf16[128,1024]{0,1:T(8,128)(2,1)S(1)}, u32[]{:S(2)}, u32[]{:S(2)}) collective-permute-start(bf16[128,1024]{0,1:T(8,128)(2,1)} %copy.95), channel_id=1, source_target_pairs={{0,4},{4,8},{8,12},{12,16},{16,20},{20,24},{24,28},{28,32},{32,36}... | collective-permute-start | bytes 786440 | tf_op jit(solution)/shard_map/while/body/eval_jaxpr/ppermute | solution.py:9
  168.4 16.8 %collective-permute-start.2 = (bf16[128,1024]{0,1:T(8,128)(2,1)}, bf16[128,1024]{0,1:T(8,128)(2,1)S(1)}, u32[]{:S(2)}, u32[]{:S(2)}) collective-permute-start(bf16[128,1024]{0,1:T(8,128)(2,1)} %copy.95), channel_id=1, source_target_pairs={{0,4},{4,8},{8,12},{12,16},{16,20},{20,24},{24,28},{28,32},{32,36}... | collective-permute-start | bytes 786440 | tf_op jit(solution)/shard_map/while/body/eval_jaxpr/ppermute | solution.py:9
  185.2 10.9 copy-start.3
  196.5 3.1 copy-start.2
  197.9 388.6 %all-gather.5.cloned.1.call-start = ((), (), s32[]{:S(2)}) async-start(), calls=%async_computation.3 | async-start | bytes 1310720 | tf_op jit(solution)/shard_map/all_gather | solution.py:143
  210.3 6.7 collective-permute-start
  232.1 6.5 collective-permute-start
  339.5 7.7 collective-permute-start
  348.0 6.9 collective-permute-start
  384.3 11.6 collective-permute-start.5
  398.1 18.4 %collective-permute-start.4 = (bf16[128,1024]{0,1:T(8,128)(2,1)S(1)}, bf16[128,1024]{0,1:T(8,128)(2,1)S(1)}, u32[]{:S(2)}, u32[]{:S(2)}) collective-permute-start(bf16[128,1024]{0,1:T(8,128)(2,1)S(1)} %get-tuple-element.1692), channel_id=1, source_target_pairs={{0,248},{4,252},{8,0},{12,4},{16,8},{20,12},{24,16},{28,20},{32,24... | collective-permute-start | bytes 786440 | tf_op jit(solution)/shard_map/ppermute | solution.py:9
  398.2 923.5 %all-reduce.3.cloned.1.call-start = ((), (), s32[]{:S(2)}) async-start(), calls=%async_computation.6 | async-start | bytes 1048576 | tf_op jit(solution)/shard_map/psum | solution.py:147
  417.3 29.6 %collective-permute-start.1 = (bf16[128,1024]{0,1:T(8,128)(2,1)}, bf16[128,1024]{0,1:T(8,128)(2,1)S(1)}, u32[]{:S(2)}, u32[]{:S(2)}) collective-permute-start(bf16[128,1024]{0,1:T(8,128)(2,1)} %copy.122), channel_id=1, source_target_pairs={{0,4},{4,8},{8,12},{12,16},{16,20},{20,24},{24,28},{28,32},{32,36}... | collective-permute-start | bytes 786440 | tf_op jit(solution)/shard_map/while/body/eval_jaxpr/ppermute | solution.py:9
  447.7 10.8 collective-permute-start.1
  459.2 94.4 %collective-permute-start.1 = (bf16[128,1024]{0,1:T(8,128)(2,1)}, bf16[128,1024]{0,1:T(8,128)(2,1)S(1)}, u32[]{:S(2)}, u32[]{:S(2)}) collective-permute-start(bf16[128,1024]{0,1:T(8,128)(2,1)} %copy.122), channel_id=1, source_target_pairs={{0,4},{4,8},{8,12},{12,16},{16,20},{20,24},{24,28},{28,32},{32,36}... | collective-permute-start | bytes 786440 | tf_op jit(solution)/shard_map/while/body/eval_jaxpr/ppermute | solution.py:9
  554.3 16.7 %collective-permute-start.1 = (bf16[128,1024]{0,1:T(8,128)(2,1)}, bf16[128,1024]{0,1:T(8,128)(2,1)S(1)}, u32[]{:S(2)}, u32[]{:S(2)}) collective-permute-start(bf16[128,1024]{0,1:T(8,128)(2,1)} %copy.122), channel_id=1, source_target_pairs={{0,4},{4,8},{8,12},{12,16},{16,20},{20,24},{24,28},{28,32},{32,36}... | collective-permute-start | bytes 786440 | tf_op jit(solution)/shard_map/while/body/eval_jaxpr/ppermute | solution.py:9
  571.0 14.2 %copy-start.1 = (bf16[512,1024]{1,0:T(8,128)(2,1)S(1)}, bf16[512,1024]{1,0:T(8,128)(2,1)}, u32[]{:S(2)}) copy-start(bf16[512,1024]{1,0:T(8,128)(2,1)} %all-gather.3.cloned.1.call-done) | copy-start | bytes 3145732
  588.8 770.4 %reduce-scatter.9.cloned.1.call-start = ((), (), s32[]{:S(2)}) async-start(), calls=%async_computation.5 | async-start | bytes 1310720
Sparse Core Ops, SparseCore 0:
  17.0 18.1 all-gather.2
  198.0 74.2 reduce-scatter.6
  398.3 118.0 all-gather.4
  588.9 732.7 all-reduce.2
  1324.9 34.1 reduce-scatter.8
where the time goes:
time: 1390 us; the launch traced here: 1370 us
  waiting for transfers between devices  824 us (59%)
  loops' own time  317 us (23%)
  local copies, waits for them, and re-layouts  82.2 us (6%)
  matrix products  70.8 us (5%)
  other arithmetic  39.9 us (3%)
  between operations  16 us (1%)
  starting transfers between devices  15.9 us (1%)
    psum x1, waiting for transfers between devices, body(): summed_first = lax.psum(first_term, 'blk')  731 us
    another operation x10, loops' own time, forward_add(): lax.fori_loop(first_place, first_place + counts[key_value], forward_one_s...  202 us
    another operation x5, loops' own time, transpose_add(): lax.fori_loop(first_place, first_place + counts[key_value], transpose_one...  100 us
    ppermute x15, waiting for transfers between devices, from_behind(): lax.ppermute(array, axis, [(i, (i + by) % peers) for i in range(peers)])  56.7 us
    dot_general x22, matrix products, forward_one_slot(): lax.dot_general(source, tiles[row, column], (((1,), (1,)), ((), ())), pre...  38.3 us
    unnamed x7, waiting for transfers between devices  35.7 us
    another operation x34, other arithmetic  32 us
  transfers between devices with their start and end apart: 20, of which 11 were waited for; matrix products, arithmetic and copies ran while one was open for 14% of the time, Pallas kernels for 0%

commit v1 on v0

v1 whole, which is shorter than its diff:
```python
import jax
import jax.numpy as jnp
from jax import lax
from jax.experimental import pallas as pl
from jax.experimental.pallas import tpu as pltpu
from jax.sharding import PartitionSpec as P

F32 = jnp.float32
BF16 = jnp.bfloat16
REACH = 2
SIDES = 2 * REACH + 1
HALO = (1, -1, 2, -2)


def behind(array, by):
    peers = lax.axis_size("blk")
    return lax.ppermute(array, "blk", [(i, (i + by) % peers) for i in range(peers)])


def across(array, flip):
    return lax.ppermute(array, "rep", [(i, i ^ flip) for i in range(lax.axis_size("rep"))])


def inverse_root(degree):
    value = jnp.float32(1.0)
    for count in range(2, 7):
        value = jnp.where(degree == count, jnp.float32(count**-0.5), value)
    return value


def place_of(slot_blocks, block_position, here, blocks, peers, row, slot):
    position = block_position[slot_blocks[row, slot]]
    side = lax.rem(position // blocks - here + REACH + peers, peers)
    return side * blocks + lax.rem(position, blocks)


def aggregate_kernel(
    peers,
    slot_blocks,
    degrees,
    block_position,
    *refs,
):
    held_refs, (tiles, weight, rows_out, keep_out, send_out, held, total) = refs[:SIDES], refs[SIDES:]
    blocks, slots, block, _ = tiles.shape
    here = lax.axis_index("blk")
    rank = lax.axis_index("rep")
    for side in range(SIDES):
        for inner in range(blocks):
            held[side * blocks + inner] = held_refs[side][:, inner * block : (inner + 1) * block]
    for row in range(blocks):
        degree = degrees[row]
        for slot in range(slots):

            def add(row=row, slot=slot):
                at = place_of(slot_blocks, block_position, here, blocks, peers, row, slot)
                part = lax.dot_general(
                    held[at],
                    tiles[row, slot],
                    (((1,), (1,)), ((), ())),
                    preferred_element_type=F32,
                )
                if slot == 0:
                    total[row] = part
                else:
                    total[row] += part

            if slot == 0:
                add()
            else:
                pl.when(slot < degree)(add)
        rows_out[:, row * block : (row + 1) * block] = (total[row] * inverse_root(degree)).astype(BF16)
    group = weight.shape[0] // 4
    rows = rows_out[...]
    for place, flip in enumerate((0, 2, 1, 3)):
        owner = rank ^ flip
        part = jnp.dot(
            weight[pl.ds(pl.multiple_of(owner * group, group), group), :],
            rows,
            preferred_element_type=F32,
        ).astype(BF16)
        out = keep_out if place < 2 else send_out
        out[(place % 2) * group : (place % 2 + 1) * group, :] = part


def spread_kernel(peers, slot_blocks, degrees, block_position, gradient, tiles, *refs):
    outs, total = refs[:SIDES], refs[SIDES]
    blocks, slots, block, _ = tiles.shape
    here = lax.axis_index("blk")
    total[...] = jnp.zeros_like(total)
    for row in range(blocks):
        degree = degrees[row]
        source = gradient[:, row * block : (row + 1) * block]
        for slot in range(slots):

            def add(row=row, slot=slot, degree=degree, source=source):
                at = place_of(slot_blocks, block_position, here, blocks, peers, row, slot)
                total[at] += jnp.dot(source, tiles[row, slot], preferred_element_type=F32) * inverse_root(degree)

            if slot == 0:
                add()
            else:
                pl.when(slot < degree)(add)
    for side in range(SIDES):
        for inner in range(blocks):
            outs[side][:, inner * block : (inner + 1) * block] = total[side * blocks + inner].astype(BF16)


SMEM = pl.BlockSpec(memory_space=pltpu.SMEM)
VMEM = pl.BlockSpec(memory_space=pltpu.VMEM)


def body(
    node_features,
    weight_first,
    weight_second,
    tiles,
    slot_blocks,
    degrees,
    block_position,
    cotangent,
):
    width, node_local = node_features.shape
    blocks, slots, block, _ = tiles.shape
    peers = lax.axis_size("blk")
    rank = lax.axis_index("rep")
    node_count = node_local * peers
    factor = node_count ** (-0.5)
    full = weight_first.shape[1]
    params = pltpu.CompilerParams(vmem_limit_bytes=40 * 1024 * 1024)
    cost = pl.CostEstimate(flops=2 * width * node_local * block * slots, bytes_accessed=8_000_000, transcendentals=0)

    def aggregate(held, weight_t):
        return pl.pallas_call(
            lambda *refs: aggregate_kernel(peers, *refs),
            out_shape=(
                jax.ShapeDtypeStruct((width, node_local), BF16),
                jax.ShapeDtypeStruct((full // 2, node_local), BF16),
                jax.ShapeDtypeStruct((full // 2, node_local), BF16),
            ),
            in_specs=[SMEM] * 3 + [VMEM] * (SIDES + 2),
            out_specs=(VMEM,) * 3,
            scratch_shapes=[
                pltpu.VMEM((SIDES * blocks, width, block), BF16),
                pltpu.VMEM((blocks, width, block), F32),
            ],
            compiler_params=params,
            cost_estimate=cost,
        )(slot_blocks, degrees, block_position, *held, tiles, weight_t)

    def halo(values):
        return [values if side == REACH else behind(values, REACH - side) for side in range(SIDES)]

    def scatter(keep, send):
        total = keep.astype(F32) + across(send, 1).astype(F32)
        other = across(total[width:].astype(BF16), 2)
        return total[:width] + other.astype(F32)

    def gather(own):
        pair = jnp.concatenate([own, across(own, 2)], axis=0)
        return jnp.concatenate([pair, across(pair, 1)], axis=0)

    def reduce_blk(term):
        parts = term.astype(BF16).reshape(width, 4, full // 4).transpose(1, 0, 2)
        parts = parts.reshape(peers, -1, full // 4)
        got = lax.all_to_all(parts, "blk", 0, 0, tiled=True)
        mine = jnp.sum(got.astype(F32), axis=0).astype(BF16)
        everyone = jnp.broadcast_to(mine[None], parts.shape)
        return lax.all_to_all(everyone, "blk", 0, 0, tiled=True).reshape(4, width, full // 4)

    def finish(groups):
        ordered = jnp.stack([lax.dynamic_index_in_dim(groups, relative_place(g), 0, keepdims=False) for g in range(4)], axis=1)
        return ordered.reshape(width, full).astype(F32) * factor

    def relative_place(group):
        flip = rank ^ group
        return (flip % 2) * 2 + flip // 2

    held_x = halo(node_features)
    parts = pl.pallas_call(
        lambda *refs: spread_kernel(peers, *refs),
        out_shape=(jax.ShapeDtypeStruct((width, node_local), BF16),) * SIDES,
        in_specs=[SMEM] * 3 + [VMEM] * 2,
        out_specs=(VMEM,) * SIDES,
        scratch_shapes=[pltpu.VMEM((SIDES * blocks, width, block), F32)],
        compiler_params=params,
        cost_estimate=cost,
    )(slot_blocks, degrees, block_position, cotangent, tiles)

    second_relative = jnp.concatenate(
        [lax.dynamic_slice_in_dim(weight_second, (rank ^ flip) * width, width, 1) for flip in (0, 2, 1, 3)], axis=1
    )
    ax_rows, keep, send = aggregate(held_x, weight_first.T)
    arrived = [parts[side] if side == REACH else behind(parts[side], side - REACH) for side in range(SIDES)]
    spread = sum(a.astype(F32) for a in arrived).astype(BF16)
    spread_all = gather(spread)
    spread_rows = jnp.dot(second_relative, spread_all, preferred_element_type=F32)

    first = scatter(keep, send)
    sigma = jax.nn.sigmoid(first)
    hidden = (first * sigma).astype(BF16)
    hidden_grad = (spread_rows * (sigma * (1.0 + first * (1.0 - sigma)))).astype(BF16)
    held_h = halo(hidden)
    _, keep_h, send_h = aggregate(held_h, weight_second.T)
    layer_output = scatter(keep_h, send_h).astype(BF16)

    term_second = lax.dot_general(hidden, spread_all, (((1,), (1,)), ((), ())), preferred_element_type=F32)
    term_first = lax.dot_general(ax_rows, gather(hidden_grad), (((1,), (1,)), ((), ())), preferred_element_type=F32)
    return layer_output, finish(reduce_blk(term_first)), finish(reduce_blk(term_second))


def solution(mesh):
    return jax.shard_map(
        body,
        mesh=mesh,
        in_specs=(
            P("rep", "blk"),
            P("rep", None),
            P("rep", None),
            P("blk", None, None, None),
            P("blk", None),
            P("blk"),
            P(),
            P("rep", "blk"),
        ),
        out_specs=(P("rep", "blk"), P("rep", None), P("rep", None)),
        check_vma=False,
    )
```

time: 1390 us -> 183 us (0.13); the launches traced: 1370 us -> 182 us
  waiting for transfers between devices: 824 us -> 75.3 us
  loops' own time: 317 us -> 0 us
  matrix products: 70.8 us -> 5.18 us
  local copies, waits for them, and re-layouts: 82.2 us -> 18.5 us
  starting transfers between devices: 15.9 us -> 65.1 us
  other arithmetic: 39.9 us -> 5.6 us
  between operations: 16 us -> 1.18 us
    psum x1 -> x0, waiting for transfers between devices: 731 us -> none  [body(): summed_first = lax.psum(first_term, 'blk')]
    another operation x18 -> x0, loops' own time: 317 us -> none  [the longest x10 202 us: forward_add(): lax.fori_loop(first_place, first_place + counts[key_value], forward_one_s...]
    dynamic_slice x101 -> x1, local copies, waits for them, and re-layouts: 70 us -> 0.02 us  [body(): lax.dynamic_slice_in_dim(weight_second, (rank ^ flip) * width, width, 1)]
    dot_general x38 -> x3, matrix products: 70.8 us -> 5.18 us  [the longest x1 1.82 us: body(): jnp.dot(second_relative, spread_all, preferred_element_type=F32)]
    all_to_all x0 -> x4, waiting for transfers between devices: none -> 39.1 us  [the longest x2 19.9 us: reduce_blk(): lax.all_to_all(everyone, 'blk', 0, 0, tiled=True)]
    unnamed x7 -> x0, waiting for transfers between devices: 35.7 us -> none
    another operation x34 -> x0, other arithmetic: 32 us -> none
    all_to_all x0 -> x4, starting transfers between devices: none -> 26.3 us  [the longest x2 15.9 us: reduce_blk(): got = lax.all_to_all(parts, 'blk', 0, 0, tiled=True)]
  transfers between devices with their start and end apart: 20 -> 24, of which waited for: 11 -> 13; matrix products, arithmetic and copies ran while one was open for 14% -> 8% of each run, Pallas kernels for 0% -> 6%
where the time goes in v1:
time: 183 us; the launch traced here: 182 us
  waiting for transfers between devices  75.3 us (41%)
  starting transfers between devices  65.1 us (36%)
  local copies, waits for them, and re-layouts  18.5 us (10%)
  Pallas kernels  11.1 us (6%)
  other arithmetic  5.6 us (3%)
  matrix products  5.18 us (3%)
    ppermute x12, starting transfers between devices, behind(): lax.ppermute(array, 'blk', [(i, (i + by) % peers) for i in range(peers)])  30.5 us
    ppermute x12, waiting for transfers between devices, behind(): lax.ppermute(array, 'blk', [(i, (i + by) % peers) for i in range(peers)])  23 us
    all_to_all x2, waiting for transfers between devices, reduce_blk(): lax.all_to_all(everyone, 'blk', 0, 0, tiled=True)  19.9 us
    all_to_all x2, waiting for transfers between devices, reduce_blk(): got = lax.all_to_all(parts, 'blk', 0, 0, tiled=True)  19.2 us
    all_to_all x2, starting transfers between devices, reduce_blk(): got = lax.all_to_all(parts, 'blk', 0, 0, tiled=True)  15.9 us
    unnamed x70, local copies, waits for them, and re-layouts  14.6 us
    ppermute x8, waiting for transfers between devices, across(): lax.ppermute(array, 'rep', [(i, i ^ flip) for i in range(lax.axis_size('r...  13.2 us
    all_to_all x2, starting transfers between devices, reduce_blk(): lax.all_to_all(everyone, 'blk', 0, 0, tiled=True)  10.4 us
  transfers between devices with their start and end apart: 24, of which 13 were waited for; matrix products, arithmetic and copies ran while one was open for 8% of the time, Pallas kernels for 6%

profile of v1, /device:TPU:8, one launch (start us, length us, event | category | flops | bytes accessed | tf_op | source)
XLA Modules:
  0.0 181.9 jit_solution(983377541956853370)
XLA Ops:
  0.6 3.3 %collective-permute-start = (bf16[128,1024]{1,0:T(8,128)(2,1)}, bf16[128,1024]{1,0:T(8,128)(2,1)S(1)}, u32[]{:S(2)}, u32[]{:S(2)}) collective-permute-start(bf16[128,1024]{1,0:T(8,128)(2,1)} %refs_5_.1), channel_id=1, source_target_pairs={{0,8},{4,12},{8,16},{12,20},{16,24},{20,28},{24,32},{28,36},{32,40... | collective-permute-start | bytes 786440 | tf_op jit(solution)/shard_map/ppermute | solution.py:17
  4.0 1.9 %collective-permute-start.1 = (bf16[128,1024]{1,0:T(8,128)(2,1)}, bf16[128,1024]{1,0:T(8,128)(2,1)S(1)}, u32[]{:S(2)}, u32[]{:S(2)}) collective-permute-start(bf16[128,1024]{1,0:T(8,128)(2,1)} %refs_5_.1), channel_id=1, source_target_pairs={{0,4},{4,8},{8,12},{12,16},{16,20},{20,24},{24,28},{28,32},{32,36}... | collective-permute-start | bytes 786440 | tf_op jit(solution)/shard_map/ppermute | solution.py:17
  5.9 4.3 %collective-permute-start.2 = (bf16[128,1024]{1,0:T(8,128)(2,1)}, bf16[128,1024]{1,0:T(8,128)(2,1)S(1)}, u32[]{:S(2)}, u32[]{:S(2)}) collective-permute-start(bf16[128,1024]{1,0:T(8,128)(2,1)} %refs_5_.1), channel_id=1, source_target_pairs={{0,252},{4,0},{8,4},{12,8},{16,12},{20,16},{24,20},{28,24},{32,28}... | collective-permute-start | bytes 786440 | tf_op jit(solution)/shard_map/ppermute | solution.py:17
  10.2 1.3 collective-permute-start.3
  11.6 1.9 %copy-done = bf16[4,6,256,256]{3,2,1,0:T(8,128)(2,1)S(1)} copy-done((bf16[4,6,256,256]{3,2,1,0:T(8,128)(2,1)S(1)}, bf16[4,6,256,256]{3,2,1,0:T(8,128)(2,1)}, u32[]{:S(2)}) %copy-start) | copy-done | bytes 3145752
  13.5 0.9 copy-done.4
  16.5 3.4 %shard_map.105 = (bf16[128,1024]{1,0:T(8,128)(2,1)}, bf16[128,1024]{1,0:T(8,128)(2,1)}, bf16[128,1024]{1,0:T(8,128)(2,1)S(1)}, bf16[128,1024]{1,0:T(8,128)(2,1)}, bf16[128,1024]{1,0:T(8,128)(2,1)}) custom-call(s32[4,6]{1,0:T(4,128)S(1)} %copy-done.14, s32[4]{0:T(128)S(1)} %copy-done.18, s32[256]{0:T(256)S(1)} %copy-done.16, bf16[128,1024]{1,0:T(8,128)(2,1)S(1)} %copy-done.4, ...), custom_call_target="tpu_custom_call" | custom-call | flops 402653184 | bytes 8000000 | tf_op jit(solution)/shard_map/pallas_call | solution.py:180
  20.5 3.0 %collective-permute-start.12 = (bf16[128,1024]{1,0:T(8,128)(2,1)}, bf16[128,1024]{1,0:T(8,128)(2,1)}, u32[]{:S(2)}, u32[]{:S(2)}) collective-permute-start(bf16[128,1024]{1,0:T(8,128)(2,1)} %get-tuple-element.18), channel_id=1, source_target_pairs={{0,248},{4,252},{8,0},{12,4},{16,8},{20,12},{24,16},{28,20},{32,24... | collective-permute-start | bytes 786440 | tf_op jit(solution)/shard_map/ppermute | solution.py:17
  24.2 1.7 collective-permute-start.13
  27.8 1.5 collective-permute-start.15
  29.3 1.0 copy.17
  30.3 4.4 %collective-permute-done.3.refs_7_ = bf16[128,1024]{1,0:T(8,128)(2,1)} collective-permute-done((bf16[128,1024]{1,0:T(8,128)(2,1)}, bf16[128,1024]{1,0:T(8,128)(2,1)}, u32[]{:S(2)}, u32[]{:S(2)}) %collective-permute-start.3) | collective-permute-done | bytes 262176 | tf_op jit(solution)/shard_map/ppermute | solution.py:17
  34.7 0.9 copy-done.7
  35.7 0.9 copy-done.9
  36.6 0.9 copy-done.11
  37.6 3.3 %shard_map.103 = (bf16[128,1024]{1,0:T(8,128)(2,1)S(1)}, bf16[256,1024]{1,0:T(8,128)(2,1)S(1)}, bf16[256,1024]{1,0:T(8,128)(2,1)S(1)}) custom-call(s32[4,6]{1,0:T(4,128)S(1)} %copy-done.15, s32[4]{0:T(128)S(1)} %copy-done.19, s32[256]{0:T(256)S(1)} %copy-done.17, bf16[128,1024]{1,0:T(8,128)(2,1)S(1)} %copy-done.7, bf16[128,1024]{1,0:T(8,128)(2,1)S(1)} %copy-done.9, ...), custom_call_target="tpu_custom_call" | custom-call | flops 402653184 | bytes 8000000 | tf_op jit(solution)/shard_map/pallas_call | solution.py:134
  41.0 3.5 %collective-permute-done.13 = bf16[128,1024]{1,0:T(8,128)(2,1)} collective-permute-done((bf16[128,1024]{1,0:T(8,128)(2,1)}, bf16[128,1024]{1,0:T(8,128)(2,1)}, u32[]{:S(2)}, u32[]{:S(2)}) %collective-permute-start.13) | collective-permute-done | bytes 262176 | tf_op jit(solution)/shard_map/ppermute | solution.py:17
  44.6 1.9 %collective-permute-done.14 = bf16[128,1024]{1,0:T(8,128)(2,1)} collective-permute-done((bf16[128,1024]{1,0:T(8,128)(2,1)}, bf16[128,1024]{1,0:T(8,128)(2,1)}, u32[]{:S(2)}, u32[]{:S(2)}) %collective-permute-start.14) | collective-permute-done | bytes 262176 | tf_op jit(solution)/shard_map/ppermute | solution.py:17
  46.5 1.4 add_convert_fusion
  47.9 2.7 %collective-permute-start.16 = (bf16[128,1024]{1,0:T(8,128)(2,1)S(1)}, bf16[128,1024]{1,0:T(8,128)(2,1)S(1)}, u32[]{:S(2)}, u32[]{:S(2)}) collective-permute-start(bf16[128,1024]{1,0:T(8,128)(2,1)S(1)} %add_convert_fusion), channel_id=1, source_target_pairs={{0,2},{1,3},{2,0},{3,1},{4,6},{5,7},{6,4},{7,5},{8,10},{9,11},{10,... | collective-permute-start | bytes 786440 | tf_op jit(solution)/shard_map/ppermute | solution.py:21
  50.6 5.3 %collective-permute-done.16 = bf16[128,1024]{1,0:T(8,128)(2,1)S(1)} collective-permute-done((bf16[128,1024]{1,0:T(8,128)(2,1)S(1)}, bf16[128,1024]{1,0:T(8,128)(2,1)S(1)}, u32[]{:S(2)}, u32[]{:S(2)}) %collective-permute-start.16) | collective-permute-done | bytes 262176 | tf_op jit(solution)/shard_map/ppermute | solution.py:21
  55.9 0.9 pad_maximum_fusion.1
  58.1 2.6 %collective-permute-start.5 = (bf16[128,1024]{1,0:T(8,128)(2,1)}, bf16[128,1024]{1,0:T(8,128)(2,1)}, u32[]{:S(2)}, u32[]{:S(2)}) collective-permute-start(bf16[128,1024]{1,0:T(8,128)(2,1)} %slice.33), channel_id=1, source_target_pairs={{0,2},{1,3},{2,0},{3,1},{4,6},{5,7},{6,4},{7,5},{8,10},{9,11},{10,... | collective-permute-start | bytes 786440 | tf_op jit(solution)/shard_map/ppermute | solution.py:21
  60.7 7.9 %collective-permute-done.5 = bf16[128,1024]{1,0:T(8,128)(2,1)} collective-permute-done((bf16[128,1024]{1,0:T(8,128)(2,1)}, bf16[128,1024]{1,0:T(8,128)(2,1)}, u32[]{:S(2)}, u32[]{:S(2)}) %collective-permute-start.5) | collective-permute-done | bytes 262176 | tf_op jit(solution)/shard_map/ppermute | solution.py:21
  68.7 1.8 %fusion = bf16[128,1024]{1,0:T(8,128)(2,1)S(1)} fusion(bf16[256,1024]{1,0:T(8,128)(2,1)} %collective-permute-done.17, bf16[128,1024]{1,0:T(8,128)(2,1)} %copy-done.27, bf16[128,1024]{1,0:T(8,128)(2,1)S(1)} %add_convert_fusion, bf16[128,1024]{1,0:T(8,128)(2,1)} %collective-permute-done.5, f32[256,1024]{1,0:T(8,128)} %copy-done.22, ...), kind=kOutput, calls=%fused_computation.1 | convolution fusion | flops 139329536 | bytes 2228224 | tf_op jit(solution)/shard_map/dot_general | solution.py:197
  70.5 2.7 %collective-permute-start.18 = (bf16[128,1024]{1,0:T(8,128)(2,1)S(1)}, bf16[128,1024]{1,0:T(8,128)(2,1)S(1)}, u32[]{:S(2)}, u32[]{:S(2)}) collective-permute-start(bf16[128,1024]{1,0:T(8,128)(2,1)S(1)} %fusion), channel_id=1, source_target_pairs={{0,2},{1,3},{2,0},{3,1},{4,6},{5,7},{6,4},{7,5},{8,10},{9,11},{10,... | collective-permute-start | bytes 786440 | tf_op jit(solution)/shard_map/ppermute | solution.py:21
  73.2 1.1 multiply_convert_fusion.refs_5_
  74.4 6.3 %collective-permute-start.7 = (bf16[128,1024]{1,0:T(8,128)(2,1)S(1)}, bf16[128,1024]{1,0:T(8,128)(2,1)}, u32[]{:S(2)}, u32[]{:S(2)}) collective-permute-start(bf16[128,1024]{1,0:T(8,128)(2,1)S(1)} %multiply_convert_fusion.refs_5_), channel_id=1, source_target_pairs={{0,4},{4,8},{8,12},{12,16},{16,20},{20,24},{24,28},{28,32},{32,36}... | collective-permute-start | bytes 786440 | tf_op jit(solution)/shard_map/ppermute | solution.py:17
  80.6 5.6 %collective-permute-start.8 = (bf16[128,1024]{1,0:T(8,128)(2,1)S(1)}, bf16[128,1024]{1,0:T(8,128)(2,1)}, u32[]{:S(2)}, u32[]{:S(2)}) collective-permute-start(bf16[128,1024]{1,0:T(8,128)(2,1)S(1)} %multiply_convert_fusion.refs_5_), channel_id=1, source_target_pairs={{0,252},{4,0},{8,4},{12,8},{16,12},{20,16},{24,20},{28,24},{32,28}... | collective-permute-start | bytes 786440 | tf_op jit(solution)/shard_map/ppermute | solution.py:17
  86.2 1.5 collective-permute-start.9
  87.7 0.9 pad_maximum_fusion.2
  88.6 1.0 copy.18
  89.6 4.6 %collective-permute-done.6.refs_3_ = bf16[128,1024]{1,0:T(8,128)(2,1)} collective-permute-done((bf16[128,1024]{1,0:T(8,128)(2,1)S(1)}, bf16[128,1024]{1,0:T(8,128)(2,1)}, u32[]{:S(2)}, u32[]{:S(2)}) %collective-permute-start.6) | collective-permute-done | bytes 262176 | tf_op jit(solution)/shard_map/ppermute | solution.py:17
  94.2 5.1 %collective-permute-done.7.refs_4_ = bf16[128,1024]{1,0:T(8,128)(2,1)} collective-permute-done((bf16[128,1024]{1,0:T(8,128)(2,1)S(1)}, bf16[128,1024]{1,0:T(8,128)(2,1)}, u32[]{:S(2)}, u32[]{:S(2)}) %collective-permute-start.7) | collective-permute-done | bytes 262176 | tf_op jit(solution)/shard_map/ppermute | solution.py:17
  99.3 3.1 %collective-permute-done.9.refs_7_ = bf16[128,1024]{1,0:T(8,128)(2,1)} collective-permute-done((bf16[128,1024]{1,0:T(8,128)(2,1)S(1)}, bf16[128,1024]{1,0:T(8,128)(2,1)}, u32[]{:S(2)}, u32[]{:S(2)}) %collective-permute-start.9) | collective-permute-done | bytes 262176 | tf_op jit(solution)/shard_map/ppermute | solution.py:17
  102.4 4.4 %shard_map.104 = (bf16[128,1024]{1,0:T(8,128)(2,1)}, bf16[256,1024]{1,0:T(8,128)(2,1)S(1)}, bf16[256,1024]{1,0:T(8,128)(2,1)}) custom-call(s32[4,6]{1,0:T(4,128)S(1)} %copy-done.15, s32[4]{0:T(128)S(1)} %copy-done.19, s32[256]{0:T(256)S(1)} %copy-done.17, bf16[128,1024]{1,0:T(8,128)(2,1)} %collective-permute-done.6.refs_3_, ...), custom_call_target="tpu_custom_call" | custom-call | flops 402653184 | bytes 8000000 | tf_op jit(solution)/shard_map/pallas_call | solution.py:134
  106.9 1.8 fusion.2
  109.4 10.8 %all-to-all-start.2 = ((bf16[64,8,128]{2,1,0:T(8,128)(2,1)}), bf16[64,8,128]{2,1,0:T(8,128)(2,1)S(1)}, u32[]{:S(2)}, u32[]{:S(2)}) async-start(bf16[64,8,128]{2,1,0:T(8,128)(2,1)} %bitcast.11), calls=%async_computation.2 | async-start | bytes 262144 | tf_op jit(solution)/shard_map/all_to_all | solution.py:166
  120.2 1.6 fusion.1
  122.5 8.7 %all-to-all-done.2 = bf16[64,8,128]{2,1,0:T(8,128)(2,1)S(1)} async-done(((bf16[64,8,128]{2,1,0:T(8,128)(2,1)}), bf16[64,8,128]{2,1,0:T(8,128)(2,1)S(1)}, u32[]{:S(2)}, u32[]{:S(2)}) %all-to-all-start.2) | async-done | bytes 131104 | tf_op jit(solution)/shard_map/all_to_all | solution.py:166
  131.2 5.1 %all-to-all-start = ((bf16[64,8,128]{2,1,0:T(8,128)(2,1)}), bf16[64,8,128]{2,1,0:T(8,128)(2,1)S(1)}, u32[]{:S(2)}, u32[]{:S(2)}) async-start(bf16[64,8,128]{2,1,0:T(8,128)(2,1)} %bitcast.3), calls=%async_computation | async-start | bytes 262144 | tf_op jit(solution)/shard_map/all_to_all | solution.py:166
  136.3 10.5 %all-to-all-done = bf16[64,8,128]{2,1,0:T(8,128)(2,1)S(1)} async-done(((bf16[64,8,128]{2,1,0:T(8,128)(2,1)}), bf16[64,8,128]{2,1,0:T(8,128)(2,1)S(1)}, u32[]{:S(2)}, u32[]{:S(2)}) %all-to-all-start) | async-done | bytes 131104 | tf_op jit(solution)/shard_map/all_to_all | solution.py:166
  147.5 5.3 %all-to-all-start.3 = ((bf16[64,8,128]{2,1,0:T(8,128)(2,1)}), bf16[64,8,128]{2,1,0:T(8,128)(2,1)S(1)}, u32[]{:S(2)}, u32[]{:S(2)}) async-start(bf16[64,8,128]{2,1,0:T(8,128)(2,1)} %broadcast_in_dim.5), calls=%async_computation.3 | async-start | bytes 262144 | tf_op jit(solution)/shard_map/all_to_all | solution.py:169
  153.2 10.2 %all-to-all-done.3 = bf16[64,8,128]{2,1,0:T(8,128)(2,1)S(1)} async-done(((bf16[64,8,128]{2,1,0:T(8,128)(2,1)}), bf16[64,8,128]{2,1,0:T(8,128)(2,1)S(1)}, u32[]{:S(2)}, u32[]{:S(2)}) %all-to-all-start.3) | async-done | bytes 131104 | tf_op jit(solution)/shard_map/all_to_all | solution.py:169
  164.1 5.2 %all-to-all-start.1 = ((bf16[64,8,128]{2,1,0:T(8,128)(2,1)}), bf16[64,8,128]{2,1,0:T(8,128)(2,1)S(1)}, u32[]{:S(2)}, u32[]{:S(2)}) async-start(bf16[64,8,128]{2,1,0:T(8,128)(2,1)} %broadcast_in_dim.4), calls=%async_computation.1 | async-start | bytes 262144 | tf_op jit(solution)/shard_map/all_to_all | solution.py:169
  170.2 9.7 %all-to-all-done.1 = bf16[64,8,128]{2,1,0:T(8,128)(2,1)S(1)} async-done(((bf16[64,8,128]{2,1,0:T(8,128)(2,1)}), bf16[64,8,128]{2,1,0:T(8,128)(2,1)S(1)}, u32[]{:S(2)}, u32[]{:S(2)}) %all-to-all-start.1) | async-done | bytes 131104 | tf_op jit(solution)/shard_map/all_to_all | solution.py:169
  180.1 0.8 copy.24
  181.1 0.8 copy.23
  (97 shorter events, 11.3 us)
Async XLA Ops:
  0.6 22.9 %collective-permute-start = (bf16[128,1024]{1,0:T(8,128)(2,1)}, bf16[128,1024]{1,0:T(8,128)(2,1)S(1)}, u32[]{:S(2)}, u32[]{:S(2)}) collective-permute-start(bf16[128,1024]{1,0:T(8,128)(2,1)} %refs_5_.1), channel_id=1, source_target_pairs={{0,8},{4,12},{8,16},{12,20},{16,24},{20,28},{24,32},{28,36},{32,40... | collective-permute-start | bytes 786440 | tf_op jit(solution)/shard_map/ppermute | solution.py:17
  4.0 22.4 %collective-permute-start.1 = (bf16[128,1024]{1,0:T(8,128)(2,1)}, bf16[128,1024]{1,0:T(8,128)(2,1)S(1)}, u32[]{:S(2)}, u32[]{:S(2)}) collective-permute-start(bf16[128,1024]{1,0:T(8,128)(2,1)} %refs_5_.1), channel_id=1, source_target_pairs={{0,4},{4,8},{8,12},{12,16},{16,20},{20,24},{24,28},{28,32},{32,36}... | collective-permute-start | bytes 786440 | tf_op jit(solution)/shard_map/ppermute | solution.py:17
  5.9 21.2 %collective-permute-start.2 = (bf16[128,1024]{1,0:T(8,128)(2,1)}, bf16[128,1024]{1,0:T(8,128)(2,1)S(1)}, u32[]{:S(2)}, u32[]{:S(2)}) collective-permute-start(bf16[128,1024]{1,0:T(8,128)(2,1)} %refs_5_.1), channel_id=1, source_target_pairs={{0,252},{4,0},{8,4},{12,8},{16,12},{20,16},{24,20},{28,24},{32,28}... | collective-permute-start | bytes 786440 | tf_op jit(solution)/shard_map/ppermute | solution.py:17
  10.2 24.5 %collective-permute-start.3 = (bf16[128,1024]{1,0:T(8,128)(2,1)}, bf16[128,1024]{1,0:T(8,128)(2,1)}, u32[]{:S(2)}, u32[]{:S(2)}) collective-permute-start(bf16[128,1024]{1,0:T(8,128)(2,1)} %refs_5_.1), channel_id=1, source_target_pairs={{0,248},{4,252},{8,0},{12,4},{16,8},{20,12},{24,16},{28,20},{32,24... | collective-permute-start | bytes 786440 | tf_op jit(solution)/shard_map/ppermute | solution.py:17
  11.6 1.9 %copy-start = (bf16[4,6,256,256]{3,2,1,0:T(8,128)(2,1)S(1)}, bf16[4,6,256,256]{3,2,1,0:T(8,128)(2,1)}, u32[]{:S(2)}) copy-start(bf16[4,6,256,256]{3,2,1,0:T(8,128)(2,1)} %refs_4_.1) | copy-start | bytes 9437188
  13.5 0.9 copy-start.4
  16.4 18.3 %copy-start.1 = (bf16[4,6,256,256]{3,2,1,0:T(8,128)(2,1)S(1)}, bf16[4,6,256,256]{3,2,1,0:T(8,128)(2,1)}, u32[]{:S(2)}) copy-start(bf16[4,6,256,256]{3,2,1,0:T(8,128)(2,1)} %refs_4_.1) | copy-start | bytes 9437188
  16.4 18.3 %copy-start.5 = (bf16[128,1024]{1,0:T(8,128)(2,1)S(1)}, bf16[128,1024]{1,0:T(8,128)(2,1)}, u32[]{:S(2)}) copy-start(bf16[128,1024]{1,0:T(8,128)(2,1)} %refs_5_.1) | copy-start | bytes 786436
  16.4 18.3 %copy-start.15 = (s32[4,6]{1,0:T(4,128)S(1)}, s32[4,6]{1,0:T(4,128)}, u32[]{:S(2)}) copy-start(s32[4,6]{1,0:T(4,128)} %refs_0_.5) | copy-start | bytes 292
  16.4 18.3 %copy-start.17 = (s32[256]{0:T(256)S(1)}, s32[256]{0:T(256)}, u32[]{:S(2)}) copy-start(s32[256]{0:T(256)} %refs_2_.5) | copy-start | bytes 3076
  16.4 18.3 %copy-start.19 = (s32[4]{0:T(128)S(1)}, s32[4]{0:T(128)}, u32[]{:S(2)}) copy-start(s32[4]{0:T(128)} %refs_1_.5) | copy-start | bytes 52
  20.5 20.5 %collective-permute-start.12 = (bf16[128,1024]{1,0:T(8,128)(2,1)}, bf16[128,1024]{1,0:T(8,128)(2,1)}, u32[]{:S(2)}, u32[]{:S(2)}) collective-permute-start(bf16[128,1024]{1,0:T(8,128)(2,1)} %get-tuple-element.18), channel_id=1, source_target_pairs={{0,248},{4,252},{8,0},{12,4},{16,8},{20,12},{24,16},{28,20},{32,24... | collective-permute-start | bytes 786440 | tf_op jit(solution)/shard_map/ppermute | solution.py:17
  24.2 20.3 %collective-permute-start.13 = (bf16[128,1024]{1,0:T(8,128)(2,1)}, bf16[128,1024]{1,0:T(8,128)(2,1)}, u32[]{:S(2)}, u32[]{:S(2)}) collective-permute-start(bf16[128,1024]{1,0:T(8,128)(2,1)} %get-tuple-element.19), channel_id=1, source_target_pairs={{0,252},{4,0},{8,4},{12,8},{16,12},{20,16},{24,20},{28,24},{32,28}... | collective-permute-start | bytes 786440 | tf_op jit(solution)/shard_map/ppermute | solution.py:17
  27.1 19.4 %collective-permute-start.14 = (bf16[128,1024]{1,0:T(8,128)(2,1)}, bf16[128,1024]{1,0:T(8,128)(2,1)}, u32[]{:S(2)}, u32[]{:S(2)}) collective-permute-start(bf16[128,1024]{1,0:T(8,128)(2,1)} %get-tuple-element.21), channel_id=1, source_target_pairs={{0,4},{4,8},{8,12},{12,16},{16,20},{20,24},{24,28},{28,32},{32,36}... | collective-permute-start | bytes 786440 | tf_op jit(solution)/shard_map/ppermute | solution.py:17
  27.8 18.7 %collective-permute-start.15 = (bf16[128,1024]{1,0:T(8,128)(2,1)}, bf16[128,1024]{1,0:T(8,128)(2,1)}, u32[]{:S(2)}, u32[]{:S(2)}) collective-permute-start(bf16[128,1024]{1,0:T(8,128)(2,1)} %get-tuple-element.22), channel_id=1, source_target_pairs={{0,8},{4,12},{8,16},{12,20},{16,24},{20,28},{24,32},{28,36},{32,40... | collective-permute-start | bytes 786440 | tf_op jit(solution)/shard_map/ppermute | solution.py:17
  34.7 1.0 copy-start.7
  35.7 0.9 copy-start.9
  36.6 0.9 copy-start.11
  37.6 8.9 %copy-start.13 = (bf16[128,1024]{1,0:T(8,128)(2,1)S(1)}, bf16[128,1024]{1,0:T(8,128)(2,1)}, u32[]{:S(2)}) copy-start(bf16[128,1024]{1,0:T(8,128)(2,1)} %copy-done.12) | copy-start | bytes 786436
  40.9 16.0 %copy-start.20 = (bf16[128,1024]{1,0:T(8,128)(2,1)}, bf16[128,1024]{1,0:T(8,128)(2,1)S(1)}, u32[]{:S(2)}) copy-start(bf16[128,1024]{1,0:T(8,128)(2,1)S(1)} %get-tuple-element.17) | copy-start | bytes 786436
  40.9 15.8 %collective-permute-start.4 = (bf16[256,1024]{1,0:T(8,128)(2,1)S(1)}, bf16[256,1024]{1,0:T(8,128)(2,1)S(1)}, u32[]{:S(2)}, u32[]{:S(2)}) collective-permute-start(bf16[256,1024]{1,0:T(8,128)(2,1)S(1)} %get-tuple-element.14), channel_id=1, source_target_pairs={{0,1},{1,0},{2,3},{3,2},{4,5},{5,4},{6,7},{7,6},{8,9},{9,8},{10,11... | collective-permute-start | bytes 1572872 | tf_op jit(solution)/shard_map/ppermute | solution.py:21
  47.9 22.6 %copy-start.24 = (bf16[128,1024]{1,0:T(8,128)(2,1)}, bf16[128,1024]{1,0:T(8,128)(2,1)S(1)}, u32[]{:S(2)}) copy-start(bf16[128,1024]{1,0:T(8,128)(2,1)S(1)} %add_convert_fusion) | copy-start | bytes 786436
  47.9 12.8 %copy-start.26 = (bf16[128,512]{1,0:T(8,128)(2,1)S(1)}, bf16[128,512]{1,0:T(8,128)(2,1)}, u32[]{:S(2)}) copy-start(bf16[128,512]{1,0:T(8,128)(2,1)} %param.10) | copy-start | bytes 393220
  47.9 8.0 %collective-permute-start.16 = (bf16[128,1024]{1,0:T(8,128)(2,1)S(1)}, bf16[128,1024]{1,0:T(8,128)(2,1)S(1)}, u32[]{:S(2)}, u32[]{:S(2)}) collective-permute-start(bf16[128,1024]{1,0:T(8,128)(2,1)S(1)} %add_convert_fusion), channel_id=1, source_target_pairs={{0,2},{1,3},{2,0},{3,1},{4,6},{5,7},{6,4},{7,5},{8,10},{9,11},{10,... | collective-permute-start | bytes 786440 | tf_op jit(solution)/shard_map/ppermute | solution.py:21
  56.8 4.0 %collective-permute-start.17 = (bf16[256,1024]{1,0:T(8,128)(2,1)}, bf16[256,1024]{1,0:T(8,128)(2,1)}, u32[]{:S(2)}, u32[]{:S(2)}) collective-permute-start(bf16[256,1024]{1,0:T(8,128)(2,1)} %pad_maximum_fusion.1), channel_id=1, source_target_pairs={{0,1},{1,0},{2,3},{3,2},{4,5},{5,4},{6,7},{7,6},{8,9},{9,8},{10,11... | collective-permute-start | bytes 1572872 | tf_op jit(solution)/shard_map/ppermute | solution.py:21
  57.0 1.1 copy-start.22
  58.1 10.5 %collective-permute-start.5 = (bf16[128,1024]{1,0:T(8,128)(2,1)}, bf16[128,1024]{1,0:T(8,128)(2,1)}, u32[]{:S(2)}, u32[]{:S(2)}) collective-permute-start(bf16[128,1024]{1,0:T(8,128)(2,1)} %slice.33), channel_id=1, source_target_pairs={{0,2},{1,3},{2,0},{3,1},{4,6},{5,7},{6,4},{7,5},{8,10},{9,11},{10,... | collective-permute-start | bytes 786440 | tf_op jit(solution)/shard_map/ppermute | solution.py:21
  68.6 4.5 %copy-start.23 = (f32[256,1024]{1,0:T(8,128)S(1)}, f32[256,1024]{1,0:T(8,128)}, u32[]{:S(2)}) copy-start(f32[256,1024]{1,0:T(8,128)} %copy-done.22) | copy-start | bytes 3145732
  70.5 18.1 %copy-start.29 = (bf16[128,1024]{1,0:T(8,128)(2,1)}, bf16[128,1024]{1,0:T(8,128)(2,1)S(1)}, u32[]{:S(2)}) copy-start(bf16[128,1024]{1,0:T(8,128)(2,1)S(1)} %fusion) | copy-start | bytes 786436
  70.5 17.2 %collective-permute-start.18 = (bf16[128,1024]{1,0:T(8,128)(2,1)S(1)}, bf16[128,1024]{1,0:T(8,128)(2,1)S(1)}, u32[]{:S(2)}, u32[]{:S(2)}) collective-permute-start(bf16[128,1024]{1,0:T(8,128)(2,1)S(1)} %fusion), channel_id=1, source_target_pairs={{0,2},{1,3},{2,0},{3,1},{4,6},{5,7},{6,4},{7,5},{8,10},{9,11},{10,... | collective-permute-start | bytes 786440 | tf_op jit(solution)/shard_map/ppermute | solution.py:21
  74.3 19.9 %collective-permute-start.6 = (bf16[128,1024]{1,0:T(8,128)(2,1)S(1)}, bf16[128,1024]{1,0:T(8,128)(2,1)}, u32[]{:S(2)}, u32[]{:S(2)}) collective-permute-start(bf16[128,1024]{1,0:T(8,128)(2,1)S(1)} %multiply_convert_fusion.refs_5_), channel_id=1, source_target_pairs={{0,8},{4,12},{8,16},{12,20},{16,24},{20,28},{24,32},{28,36},{32,40... | collective-permute-start | bytes 786440 | tf_op jit(solution)/shard_map/ppermute | solution.py:17
  74.4 24.9 %collective-permute-start.7 = (bf16[128,1024]{1,0:T(8,128)(2,1)S(1)}, bf16[128,1024]{1,0:T(8,128)(2,1)}, u32[]{:S(2)}, u32[]{:S(2)}) collective-permute-start(bf16[128,1024]{1,0:T(8,128)(2,1)S(1)} %multiply_convert_fusion.refs_5_), channel_id=1, source_target_pairs={{0,4},{4,8},{8,12},{12,16},{16,20},{20,24},{24,28},{28,32},{32,36}... | collective-permute-start | bytes 786440 | tf_op jit(solution)/shard_map/ppermute | solution.py:17
  80.6 18.7 %collective-permute-start.8 = (bf16[128,1024]{1,0:T(8,128)(2,1)S(1)}, bf16[128,1024]{1,0:T(8,128)(2,1)}, u32[]{:S(2)}, u32[]{:S(2)}) collective-permute-start(bf16[128,1024]{1,0:T(8,128)(2,1)S(1)} %multiply_convert_fusion.refs_5_), channel_id=1, source_target_pairs={{0,252},{4,0},{8,4},{12,8},{16,12},{20,16},{24,20},{28,24},{32,28}... | collective-permute-start | bytes 786440 | tf_op jit(solution)/shard_map/ppermute | solution.py:17
  86.2 16.1 %collective-permute-start.9 = (bf16[128,1024]{1,0:T(8,128)(2,1)S(1)}, bf16[128,1024]{1,0:T(8,128)(2,1)}, u32[]{:S(2)}, u32[]{:S(2)}) collective-permute-start(bf16[128,1024]{1,0:T(8,128)(2,1)S(1)} %multiply_convert_fusion.refs_5_), channel_id=1, source_target_pairs={{0,248},{4,252},{8,0},{12,4},{16,8},{20,12},{24,16},{28,20},{32,24... | collective-permute-start | bytes 786440 | tf_op jit(solution)/shard_map/ppermute | solution.py:17
  88.6 31.6 %collective-permute-start.19 = (bf16[256,1024]{1,0:T(8,128)(2,1)}, bf16[256,1024]{1,0:T(8,128)(2,1)}, u32[]{:S(2)}, u32[]{:S(2)}) collective-permute-start(bf16[256,1024]{1,0:T(8,128)(2,1)} %pad_maximum_fusion.2), channel_id=1, source_target_pairs={{0,1},{1,0},{2,3},{3,2},{4,5},{5,4},{6,7},{7,6},{8,9},{9,8},{10,11... | collective-permute-start | bytes 1572872 | tf_op jit(solution)/shard_map/ppermute | solution.py:21
  102.4 4.5 %copy-start.25 = (bf16[128,1024]{1,0:T(8,128)(2,1)S(1)}, bf16[128,1024]{1,0:T(8,128)(2,1)}, u32[]{:S(2)}) copy-start(bf16[128,1024]{1,0:T(8,128)(2,1)} %copy-done.24) | copy-start | bytes 786436
  102.4 4.5 %copy-start.28 = (bf16[128,1024]{1,0:T(8,128)(2,1)S(1)}, bf16[128,1024]{1,0:T(8,128)(2,1)}, u32[]{:S(2)}) copy-start(bf16[128,1024]{1,0:T(8,128)(2,1)} %copy-done.27) | copy-start | bytes 786436
  106.8 1.9 %copy-start.2 = (bf16[256,1024]{1,0:T(8,128)(2,1)}, bf16[256,1024]{1,0:T(8,128)(2,1)S(1)}, u32[]{:S(2)}) copy-start(bf16[256,1024]{1,0:T(8,128)(2,1)S(1)} %get-tuple-element.15) | copy-start | bytes 1572868
  106.8 13.4 %copy-start.21 = (bf16[128,1024]{1,0:T(8,128)(2,1)S(1)}, bf16[128,1024]{1,0:T(8,128)(2,1)}, u32[]{:S(2)}) copy-start(bf16[128,1024]{1,0:T(8,128)(2,1)} %copy-done.20) | copy-start | bytes 786436
  106.8 13.4 %copy-start.30 = (bf16[128,1024]{1,0:T(8,128)(2,1)S(1)}, bf16[128,1024]{1,0:T(8,128)(2,1)}, u32[]{:S(2)}) copy-start(bf16[128,1024]{1,0:T(8,128)(2,1)} %copy-done.29) | copy-start | bytes 786436
  106.8 13.4 %copy-start.32 = (bf16[128,1024]{1,0:T(8,128)(2,1)S(1)}, bf16[128,1024]{1,0:T(8,128)(2,1)}, u32[]{:S(2)}) copy-start(bf16[128,1024]{1,0:T(8,128)(2,1)} %copy-done.31) | copy-start | bytes 786436
  106.8 46.0 %collective-permute-start.10 = (bf16[256,1024]{1,0:T(8,128)(2,1)}, bf16[256,1024]{1,0:T(8,128)(2,1)S(1)}, u32[]{:S(2)}, u32[]{:S(2)}) collective-permute-start(bf16[256,1024]{1,0:T(8,128)(2,1)} %get-tuple-element.16), channel_id=1, source_target_pairs={{0,1},{1,0},{2,3},{3,2},{4,5},{5,4},{6,7},{7,6},{8,9},{9,8},{10,11... | collective-permute-start | bytes 1572872 | tf_op jit(solution)/shard_map/ppermute | solution.py:21
  109.4 21.8 %all-to-all-start.2 = ((bf16[64,8,128]{2,1,0:T(8,128)(2,1)}), bf16[64,8,128]{2,1,0:T(8,128)(2,1)S(1)}, u32[]{:S(2)}, u32[]{:S(2)}) async-start(bf16[64,8,128]{2,1,0:T(8,128)(2,1)} %bitcast.11), calls=%async_computation.2 | async-start | bytes 262144 | tf_op jit(solution)/shard_map/all_to_all | solution.py:166
  120.2 32.6 %copy-start.3 = (bf16[256,1024]{1,0:T(8,128)(2,1)S(1)}, bf16[256,1024]{1,0:T(8,128)(2,1)}, u32[]{:S(2)}) copy-start(bf16[256,1024]{1,0:T(8,128)(2,1)} %copy-done.2) | copy-start | bytes 1572868
  131.2 15.7 %all-to-all-start = ((bf16[64,8,128]{2,1,0:T(8,128)(2,1)}), bf16[64,8,128]{2,1,0:T(8,128)(2,1)S(1)}, u32[]{:S(2)}, u32[]{:S(2)}) async-start(bf16[64,8,128]{2,1,0:T(8,128)(2,1)} %bitcast.3), calls=%async_computation | async-start | bytes 262144 | tf_op jit(solution)/shard_map/all_to_all | solution.py:166
  147.5 15.9 %all-to-all-start.3 = ((bf16[64,8,128]{2,1,0:T(8,128)(2,1)}), bf16[64,8,128]{2,1,0:T(8,128)(2,1)S(1)}, u32[]{:S(2)}, u32[]{:S(2)}) async-start(bf16[64,8,128]{2,1,0:T(8,128)(2,1)} %broadcast_in_dim.5), calls=%async_computation.3 | async-start | bytes 262144 | tf_op jit(solution)/shard_map/all_to_all | solution.py:169
  153.1 16.4 %collective-permute-start.11 = (bf16[128,1024]{1,0:T(8,128)(2,1)S(1)}, bf16[128,1024]{1,0:T(8,128)(2,1)S(1)}, u32[]{:S(2)}, u32[]{:S(2)}) collective-permute-start(bf16[128,1024]{1,0:T(8,128)(2,1)S(1)} %slice.32), channel_id=1, source_target_pairs={{0,2},{1,3},{2,0},{3,1},{4,6},{5,7},{6,4},{7,5},{8,10},{9,11},{10,... | collective-permute-start | bytes 786440 | tf_op jit(solution)/shard_map/ppermute | solution.py:21
  164.1 15.8 %all-to-all-start.1 = ((bf16[64,8,128]{2,1,0:T(8,128)(2,1)}), bf16[64,8,128]{2,1,0:T(8,128)(2,1)S(1)}, u32[]{:S(2)}, u32[]{:S(2)}) async-start(bf16[64,8,128]{2,1,0:T(8,128)(2,1)} %broadcast_in_dim.4), calls=%async_computation.1 | async-start | bytes 262144 | tf_op jit(solution)/shard_map/all_to_all | solution.py:169
  (9 other events, 6.6 us)

commit v2 on v1

v2 whole, which is shorter than its diff:
```python
import jax
import jax.numpy as jnp
from jax import lax
from jax.experimental import pallas as pl
from jax.experimental.pallas import tpu as pltpu
from jax.sharding import PartitionSpec as P

F32 = jnp.float32
BF16 = jnp.bfloat16
REACH = 2
SIDES = 2 * REACH + 1
FAR_FIRST = (0, 4, 1, 3)
FLIPS = (0, 2, 1, 3)


def behind(array, by):
    peers = lax.axis_size("blk")
    return lax.ppermute(array, "blk", [(i, (i + by) % peers) for i in range(peers)])


def across(array, flip):
    return lax.ppermute(array, "rep", [(i, i ^ flip) for i in range(lax.axis_size("rep"))])


def inverse_root(degree):
    value = jnp.float32(1.0)
    for count in range(2, 7):
        value = jnp.where(degree == count, jnp.float32(count**-0.5), value)
    return value


def place_of(slot_blocks, block_position, here, blocks, peers, row, slot):
    position = block_position[slot_blocks[row, slot]]
    side = lax.rem(position // blocks - here + REACH + peers, peers)
    return side * blocks + lax.rem(position, blocks)


def mix_rows(rank, weight, rows, keep_out, send_out):
    group = weight.shape[1] // 4
    for place, flip in enumerate(FLIPS):
        owner = rank ^ flip
        part = lax.dot_general(
            weight[:, pl.ds(pl.multiple_of(owner * group, group), group)],
            rows,
            (((0,), (0,)), ((), ())),
            preferred_element_type=F32,
        ).astype(BF16)
        out = keep_out if place < 2 else send_out
        out[(place % 2) * group : (place % 2 + 1) * group, :] = part


def gather_rows(peers, slot_blocks, degrees, block_position, tiles, held, total, rows_out):
    blocks, slots, block, _ = tiles.shape
    here = lax.axis_index("blk")
    for row in range(blocks):
        degree = degrees[row]
        for slot in range(slots):

            def add(row=row, slot=slot):
                at = place_of(slot_blocks, block_position, here, blocks, peers, row, slot)
                part = lax.dot_general(
                    held[at],
                    tiles[row, slot],
                    (((1,), (1,)), ((), ())),
                    preferred_element_type=F32,
                )
                if slot == 0:
                    total[row] = part
                else:
                    total[row] += part

            if slot == 0:
                add()
            else:
                pl.when(slot < degree)(add)
        rows_out[:, row * block : (row + 1) * block] = (total[row] * inverse_root(degree)).astype(BF16)


def join_kernel(ahead, back, part_ahead, part_back, join_ahead, join_back):
    width = ahead.shape[0]
    join_ahead[:width] = ahead[...]
    join_ahead[width:] = part_ahead[...]
    join_back[:width] = back[...]
    join_back[width:] = part_back[...]


def relay_kernel(part_ahead, part_back, far_ahead, far_back, sum_ahead, sum_back):
    width = sum_ahead.shape[0]
    sum_ahead[...] = (part_ahead[...].astype(F32) + far_ahead[width:].astype(F32)).astype(BF16)
    sum_back[...] = (part_back[...].astype(F32) + far_back[width:].astype(F32)).astype(BF16)


def add_kernel(part, came_ahead, came_back, spread):
    total = part[...].astype(F32) + came_ahead[...].astype(F32) + came_back[...].astype(F32)
    spread[...] = total.astype(BF16)


def first_kernel(peers, slot_blocks, degrees, block_position, *refs):
    far_ahead, near_ahead, own, near_back, far_back = refs[:5]
    tiles, weight, rows_out, keep_out, send_out, held, total = refs[5:]
    blocks, _, block, _ = tiles.shape
    width = own.shape[0]
    for side, ref in enumerate((far_ahead, near_ahead, own, near_back, far_back)):
        for inner in range(blocks):
            held[side * blocks + inner] = ref[:width, inner * block : (inner + 1) * block]
    gather_rows(peers, slot_blocks, degrees, block_position, tiles, held, total, rows_out)
    mix_rows(lax.axis_index("rep"), weight, rows_out[...], keep_out, send_out)


def second_kernel(peers, slot_blocks, degrees, block_position, *refs):
    held_refs, (tiles, weight, keep_out, send_out, held, total, rows) = refs[:SIDES], refs[SIDES:]
    blocks, _, block, _ = tiles.shape
    for side in range(SIDES):
        for inner in range(blocks):
            held[side * blocks + inner] = held_refs[side][:, inner * block : (inner + 1) * block]
    gather_rows(peers, slot_blocks, degrees, block_position, tiles, held, total, rows)
    mix_rows(lax.axis_index("rep"), weight, rows[...], keep_out, send_out)


def spread_kernel(peers, slot_blocks, degrees, block_position, gradient, tiles, *refs):
    outs, (gradient_in, tiles_in, total, sem, row_sems) = refs[:SIDES], refs[SIDES:]
    blocks, slots, block, _ = tiles.shape
    here = lax.axis_index("blk")
    copy = pltpu.make_async_copy(gradient, gradient_in, sem)
    rows = [pltpu.make_async_copy(tiles.at[row], tiles_in.at[row], row_sems.at[row]) for row in range(blocks)]
    for started in (copy, *rows):
        started.start()
    total[...] = jnp.zeros_like(total)
    copy.wait()
    for row in range(blocks):
        degree = degrees[row]
        source = gradient_in[:, row * block : (row + 1) * block]
        rows[row].wait()
        for slot in range(slots):

            def add(row=row, slot=slot, degree=degree, source=source):
                at = place_of(slot_blocks, block_position, here, blocks, peers, row, slot)
                total[at] += jnp.dot(source, tiles_in[row, slot], preferred_element_type=F32) * inverse_root(degree)

            if slot == 0:
                add()
            else:
                pl.when(slot < degree)(add)
    for side in range(SIDES):
        for inner in range(blocks):
            outs[side][:, inner * block : (inner + 1) * block] = total[side * blocks + inner].astype(BF16)


def settle_kernel(keep, came, mine, other):
    width = mine.shape[0]
    mine[...] = keep[:width].astype(F32) + came[:width].astype(F32)
    other[...] = (keep[width:].astype(F32) + came[width:].astype(F32)).astype(BF16)


def activate_kernel(mine, came, hidden, slope):
    first = mine[...] + came[: mine.shape[0]].astype(F32)
    sigma = 1.0 / (1.0 + jnp.exp(-first))
    hidden[...] = (first * sigma).astype(BF16)
    slope[...] = sigma * (1.0 + first * (1.0 - sigma))


def back_kernel(weight, slope, hidden, *refs):
    spread, (grad, term) = refs[:4], refs[4:]
    rank = lax.axis_index("rep")
    width = hidden.shape[0]
    total = None
    for place, flip in enumerate(FLIPS):
        owner = rank ^ flip
        part = jnp.dot(
            weight[:, pl.ds(pl.multiple_of(owner * width, width), width)],
            spread[place][...],
            preferred_element_type=F32,
        )
        total = part if place == 0 else total + part
    grad[...] = (total * slope[...]).astype(BF16)
    for place in range(4):
        term[place * width : (place + 1) * width] = lax.dot_general(
            hidden[...], spread[place][...], (((1,), (1,)), ((), ())), preferred_element_type=F32
        ).astype(BF16)


def outer_kernel(rows, term_second, *refs):
    grads, out = refs[:4], refs[4]
    width = rows.shape[0]
    for place in range(4):
        out[place * width : (place + 1) * width] = lax.dot_general(
            rows[...], grads[place][...], (((1,), (1,)), ((), ())), preferred_element_type=F32
        ).astype(BF16)
    out[4 * width :] = term_second[...]


def chunk_kernel(got, out):
    rows = 16
    total = got[:rows].astype(F32)
    for peer in range(1, got.shape[0] // rows):
        total += got[peer * rows : (peer + 1) * rows].astype(F32)
    block = total.astype(BF16)
    for peer in range(out.shape[0] // rows):
        out[peer * rows : (peer + 1) * rows] = block


def finish_kernel(factor, chunks, first, second):
    rank = lax.axis_index("rep")
    width = first.shape[0]
    for index, out in enumerate((first, second)):
        for place, flip in enumerate(FLIPS):
            at = index * 4 + place
            columns = pl.ds(pl.multiple_of((rank ^ flip) * width, width), width)
            out[:, columns] = chunks[at * width : (at + 1) * width].astype(F32) * factor


SMEM = pl.BlockSpec(memory_space=pltpu.SMEM)
VMEM = pl.BlockSpec(memory_space=pltpu.VMEM)
ANY = pl.BlockSpec(memory_space=pl.ANY)
MIB = 1024 * 1024


def body(
    node_features,
    weight_first,
    weight_second,
    tiles,
    slot_blocks,
    degrees,
    block_position,
    cotangent,
):
    width, node_local = node_features.shape
    blocks, slots, block, _ = tiles.shape
    peers = lax.axis_size("blk")
    factor = (node_local * peers) ** (-0.5)
    full = weight_first.shape[1]
    lists = (slot_blocks, degrees, block_position)
    node = jax.ShapeDtypeStruct((width, node_local), BF16)
    node_wide = jax.ShapeDtypeStruct((width, node_local), F32)
    half = jax.ShapeDtypeStruct((full // 2, node_local), BF16)

    def call(kernel, outs, in_specs, *args, scratch=(), out_specs=None, aliases={}, limit=12):
        return pl.pallas_call(
            kernel,
            out_shape=outs,
            in_specs=in_specs,
            out_specs=out_specs or jax.tree.map(lambda _: VMEM, outs),
            input_output_aliases=aliases,
            scratch_shapes=list(scratch),
            compiler_params=pltpu.CompilerParams(vmem_limit_bytes=limit * MIB),
            cost_estimate=pl.CostEstimate(flops=0, bytes_accessed=0, transcendentals=0),
        )(*args)

    def halo(values):
        held = {side: behind(values, REACH - side) for side in FAR_FIRST}
        held[REACH] = values
        return [held[side] for side in range(SIDES)]

    def gather(own, far):
        return own, far, across(own, 1), across(far, 1)

    pair = jax.ShapeDtypeStruct((2 * width, node_local), BF16)
    near_ahead = behind(node_features, 1)
    near_back = behind(node_features, -1)
    parts = call(
        lambda *refs: spread_kernel(peers, *refs),
        (node,) * SIDES,
        [SMEM] * 3 + [ANY] * 2,
        *lists,
        cotangent,
        tiles,
        scratch=[
            pltpu.VMEM((width, node_local), BF16),
            pltpu.VMEM(tiles.shape, BF16),
            pltpu.VMEM((SIDES * blocks, width, block), F32),
            pltpu.SemaphoreType.DMA,
            pltpu.SemaphoreType.DMA((blocks,)),
        ],
    )
    joined = call(join_kernel, (pair, pair), [VMEM] * 4, near_ahead, near_back, parts[4], parts[0])
    far_ahead, far_back = behind(joined[0], 1), behind(joined[1], -1)
    sums = call(relay_kernel, (node, node), [VMEM] * 4, parts[3], parts[1], far_ahead, far_back)
    came_ahead, came_back = behind(sums[0], 1), behind(sums[1], -1)
    held_scratch = [
        pltpu.VMEM((SIDES * blocks, width, block), BF16),
        pltpu.VMEM((blocks, width, block), F32),
    ]
    spread = call(add_kernel, node, [VMEM] * 3, parts[REACH], came_ahead, came_back)
    ax_rows, keep, send = call(
        lambda _, *refs: first_kernel(peers, *refs),
        (node, half, half),
        [ANY] + [SMEM] * 3 + [VMEM] * 7,
        spread,
        *lists,
        far_ahead,
        near_ahead,
        node_features,
        near_back,
        far_back,
        tiles,
        weight_first,
        scratch=held_scratch,
        limit=16,
    )
    mine, other = call(settle_kernel, (node_wide, node), [VMEM] * 2, keep, across(send, 1))
    came = across(other, 2)
    spread_all = gather(spread, across(spread, 2))
    hidden, slope = call(activate_kernel, (node, node_wide), [VMEM] * 2, mine, came)
    held_h = halo(hidden)
    hidden_grad, term_second = call(
        back_kernel,
        (node, jax.ShapeDtypeStruct((full, full // 4), BF16)),
        [VMEM] * 7,
        weight_second,
        slope,
        hidden,
        *spread_all,
    )
    stacked = jax.ShapeDtypeStruct((2 * full, full // 4), BF16)
    grad_all = gather(hidden_grad, across(hidden_grad, 2))
    terms = call(outer_kernel, stacked, [VMEM] * 6, ax_rows, term_second, *grad_all)
    got = lax.all_to_all(terms, "blk", 0, 0, tiled=True)
    chunks = call(chunk_kernel, stacked, [VMEM], got)
    everyone = lax.all_to_all(chunks, "blk", 0, 0, tiled=True)
    keep_h, send_h = call(
        lambda *refs: second_kernel(peers, *refs),
        (half, half),
        [SMEM] * 3 + [VMEM] * (SIDES + 2),
        *lists,
        *held_h,
        tiles,
        weight_second,
        scratch=[*held_scratch, pltpu.VMEM((width, node_local), BF16)],
    )
    mine_h, other_h = call(
        settle_kernel, (node_wide, node), [VMEM] * 2, keep_h, across(send_h, 1)
    )
    came_h = across(other_h, 2)
    layer_output = (mine_h + came_h.astype(F32)).astype(BF16)

    grad = jax.ShapeDtypeStruct((width, full), F32)
    first_out, second_out = call(lambda *refs: finish_kernel(factor, *refs), (grad, grad), [VMEM], everyone)
    return layer_output, first_out, second_out


def solution(mesh):
    return jax.shard_map(
        body,
        mesh=mesh,
        in_specs=(
            P("rep", "blk"),
            P("rep", None),
            P("rep", None),
            P("blk", None, None, None),
            P("blk", None),
            P("blk"),
            P(),
            P("rep", "blk"),
        ),
        out_specs=(P("rep", "blk"), P("rep", None), P("rep", None)),
        check_vma=False,
    )
```

time: 183 us -> 137 us (0.75)
  starting transfers between devices: 65.1 us -> 43 us
  blocking collectives: 0 us -> 21.2 us
  waiting for transfers between devices: 75.3 us -> 54.4 us
  local copies, waits for them, and re-layouts: 18.5 us -> 4.88 us
  matrix products: 5.18 us -> 0 us
  other arithmetic: 5.6 us -> 0.76 us
    all_to_all x4 -> x1, waiting for transfers between devices: 39.1 us -> 0.85 us  [body(): everyone = lax.all_to_all(chunks, 'blk', 0, 0, tiled=True)]
    all_to_all x4 -> x1, starting transfers between devices: 26.3 us -> 4.88 us  [body(): everyone = lax.all_to_all(chunks, 'blk', 0, 0, tiled=True)]
    all_to_all x0 -> x1, blocking collectives: none -> 21.2 us  [body(): got = lax.all_to_all(terms, 'blk', 0, 0, tiled=True)]
    unnamed x70 -> x24, local copies, waits for them, and re-layouts: 14.6 us -> 4.88 us
    ppermute x12 -> x10, waiting for transfers between devices: 23 us -> 32.6 us  [behind(): lax.ppermute(array, 'blk', [(i, (i + by) % peers) for i in range(peers)])]
    ppermute x8 -> x10, waiting for transfers between devices: 13.2 us -> 21 us  [across(): lax.ppermute(array, 'rep', [(i, i ^ flip) for i in range(lax.axis_size('r...]
    dot_general x3 -> x0, matrix products: 5.18 us -> none  [the longest x1 1.82 us: body(): jnp.dot(second_relative, spread_all, preferred_element_type=F32)]
    convert_element_type x3 -> x1, other arithmetic: 3.27 us -> 0.76 us  [body(): layer_output = (mine_h + came_h.astype(F32)).astype(BF16)]
  transfers between devices with their start and end apart: 24 -> 21, of which waited for: 13 -> 9; matrix products, arithmetic and copies ran while one was open for 8% -> 1% of each run, Pallas kernels for 6% -> 5%
where the time goes in v2:
time: 137 us
  waiting for transfers between devices  54.4 us (40%)
  starting transfers between devices  43 us (31%)
  blocking collectives  21.2 us (15%)
  Pallas kernels  11.9 us (9%)
  local copies, waits for them, and re-layouts  4.88 us (4%)
    ppermute x10, waiting for transfers between devices, behind(): lax.ppermute(array, 'blk', [(i, (i + by) % peers) for i in range(peers)])  32.6 us
    ppermute x10, starting transfers between devices, behind(): lax.ppermute(array, 'blk', [(i, (i + by) % peers) for i in range(peers)])  29.4 us
    all_to_all x1, blocking collectives, body(): got = lax.all_to_all(terms, 'blk', 0, 0, tiled=True)  21.2 us
    ppermute x10, waiting for transfers between devices, across(): lax.ppermute(array, 'rep', [(i, i ^ flip) for i in range(lax.axis_size('r...  21 us
    pallas_call x13, Pallas kernels, call(): pl.pallas_call(kernel, out_shape=outs, in_specs=in_specs, out_specs=out_s...  11.9 us
    ppermute x10, starting transfers between devices, across(): lax.ppermute(array, 'rep', [(i, i ^ flip) for i in range(lax.axis_size('r...  8.76 us
    unnamed x24, local copies, waits for them, and re-layouts  4.88 us
    all_to_all x1, starting transfers between devices, body(): everyone = lax.all_to_all(chunks, 'blk', 0, 0, tiled=True)  4.88 us
  transfers between devices with their start and end apart: 21, of which 9 were waited for; matrix products, arithmetic and copies ran while one was open for 1% of the time, Pallas kernels for 5%

profile of v2, /device:TPU:8, one launch (start us, length us, event | category | flops | bytes accessed | tf_op | source)
XLA Modules:
  0.0 137.1 jit_solution(13676821585292267453)
XLA Ops:
  0.6 2.0 %collective-permute-start = (bf16[128,1024]{1,0:T(8,128)(2,1)}, bf16[128,1024]{1,0:T(8,128)(2,1)S(1)}, u32[]{:S(2)}, u32[]{:S(2)}) collective-permute-start(bf16[128,1024]{1,0:T(8,128)(2,1)} %refs_5_.1), channel_id=1, source_target_pairs={{0,4},{4,8},{8,12},{12,16},{16,20},{20,24},{24,28},{28,32},{32,36}... | collective-permute-start | bytes 786440 | tf_op jit(solution)/shard_map/ppermute | solution.py:18
  2.6 6.1 %collective-permute-start.1 = (bf16[128,1024]{1,0:T(8,128)(2,1)}, bf16[128,1024]{1,0:T(8,128)(2,1)S(1)}, u32[]{:S(2)}, u32[]{:S(2)}) collective-permute-start(bf16[128,1024]{1,0:T(8,128)(2,1)} %refs_5_.1), channel_id=1, source_target_pairs={{0,252},{4,0},{8,4},{12,8},{16,12},{20,16},{24,20},{28,24},{32,28}... | collective-permute-start | bytes 786440 | tf_op jit(solution)/shard_map/ppermute | solution.py:18
  8.7 1.9 %copy-done = bf16[4,6,256,256]{3,2,1,0:T(8,128)(2,1)S(1)} copy-done((bf16[4,6,256,256]{3,2,1,0:T(8,128)(2,1)S(1)}, bf16[4,6,256,256]{3,2,1,0:T(8,128)(2,1)}, u32[]{:S(2)}) %copy-start) | copy-done | bytes 3145752
  10.6 0.9 copy-done.3
  11.6 0.7 copy-done.6
  12.3 0.7 copy-done.8
  12.9 0.7 copy-done.10
  13.6 2.8 %shard_map.103 = (bf16[128,1024]{1,0:T(8,128)(2,1)S(1)}, bf16[128,1024]{1,0:T(8,128)(2,1)S(1)}, bf16[128,1024]{1,0:T(8,128)(2,1)S(1)}, bf16[128,1024]{1,0:T(8,128)(2,1)S(1)}, bf16[128,1024]{1,0:T(8,128)(2,1)S(1)}) custom-call(s32[4,6]{1,0:T(4,128)S(1)} %copy-done.6, s32[4]{0:T(128)S(1)} %copy-done.10, s32[256]{0:T(256)S(1)} %copy-done.8, ...), custom_call_target="tpu_custom_call" | custom-call | tf_op jit(solution)/shard_map/pallas_call | solution.py:239
  16.4 0.0 collective-permute-done.1.back.refs_6_
  16.5 0.1 shard_map.104
  16.5 0.1 collective-permute-start.2
  16.6 6.2 %collective-permute-start.3 = (bf16[256,1024]{1,0:T(8,128)(2,1)S(1)}, bf16[256,1024]{1,0:T(8,128)(2,1)S(1)}, u32[]{:S(2)}, u32[]{:S(2)}) collective-permute-start(bf16[256,1024]{1,0:T(8,128)(2,1)S(1)} %get-tuple-element.33), channel_id=1, source_target_pairs={{0,252},{4,0},{8,4},{12,8},{16,12},{20,16},{24,20},{28,24},{32,28}... | collective-permute-start | bytes 1572872 | tf_op jit(solution)/shard_map/ppermute | solution.py:18
  22.9 11.4 %collective-permute-done.2.far_ahead.refs_3_ = bf16[256,1024]{1,0:T(8,128)(2,1)S(1)} collective-permute-done((bf16[256,1024]{1,0:T(8,128)(2,1)S(1)}, bf16[256,1024]{1,0:T(8,128)(2,1)S(1)}, u32[]{:S(2)}, u32[]{:S(2)}) %collective-permute-start.2) | collective-permute-done | bytes 524320 | tf_op jit(solution)/shard_map/ppermute | solution.py:18
  34.2 0.1 shard_map.105
  34.3 0.1 collective-permute-start.4
  34.4 6.2 %collective-permute-start.5 = (bf16[128,1024]{1,0:T(8,128)(2,1)S(1)}, bf16[128,1024]{1,0:T(8,128)(2,1)S(1)}, u32[]{:S(2)}, u32[]{:S(2)}) collective-permute-start(bf16[128,1024]{1,0:T(8,128)(2,1)S(1)} %get-tuple-element.35), channel_id=1, source_target_pairs={{0,252},{4,0},{8,4},{12,8},{16,12},{20,16},{24,20},{28,24},{32,28}... | collective-permute-start | bytes 786440 | tf_op jit(solution)/shard_map/ppermute | solution.py:18
  40.7 4.8 %collective-permute-done.4.came_ahead = bf16[128,1024]{1,0:T(8,128)(2,1)S(1)} collective-permute-done((bf16[128,1024]{1,0:T(8,128)(2,1)S(1)}, bf16[128,1024]{1,0:T(8,128)(2,1)S(1)}, u32[]{:S(2)}, u32[]{:S(2)}) %collective-permute-start.4) | collective-permute-done | bytes 262176 | tf_op jit(solution)/shard_map/ppermute | solution.py:18
  45.5 0.1 shard_map.106._.refs_0_
  45.7 0.0 copy-start.2
  45.7 2.8 %shard_map.107 = (bf16[128,1024]{1,0:T(8,128)(2,1)S(1)}, bf16[256,1024]{1,0:T(8,128)(2,1)S(1)}, bf16[256,1024]{1,0:T(8,128)(2,1)S(1)}) custom-call(bf16[128,1024]{1,0:T(8,128)(2,1)S(1)} %shard_map.106._.refs_0_, s32[4,6]{1,0:T(4,128)S(1)} %copy-done.7, s32[4]{0:T(128)S(1)} %copy-done.11, s32[256]{0:T(256)S(1)} %copy-done.9, ...), custom_call_target="tpu_custom_call" | custom-call | tf_op jit(solution)/shard_map/pallas_call | solution.py:239
  48.4 0.1 collective-permute-start.6
  48.5 2.7 %collective-permute-start.14 = (bf16[128,1024]{1,0:T(8,128)(2,1)S(1)}, bf16[128,1024]{1,0:T(8,128)(2,1)S(1)}, u32[]{:S(2)}, u32[]{:S(2)}) collective-permute-start(bf16[128,1024]{1,0:T(8,128)(2,1)S(1)} %shard_map.106._.refs_0_), channel_id=1, source_target_pairs={{0,2},{1,3},{2,0},{3,1},{4,6},{5,7},{6,4},{7,5},{8,10},{9,11},{10,... | collective-permute-start | bytes 786440 | tf_op jit(solution)/shard_map/ppermute | solution.py:22
  51.2 0.1 shard_map.108
  51.4 1.9 %collective-permute-start.7 = (bf16[128,1024]{1,0:T(8,128)(2,1)S(1)}, bf16[128,1024]{1,0:T(8,128)(2,1)S(1)}, u32[]{:S(2)}, u32[]{:S(2)}) collective-permute-start(bf16[128,1024]{1,0:T(8,128)(2,1)S(1)} %get-tuple-element.39), channel_id=1, source_target_pairs={{0,2},{1,3},{2,0},{3,1},{4,6},{5,7},{6,4},{7,5},{8,10},{9,11},{10,... | collective-permute-start | bytes 786440 | tf_op jit(solution)/shard_map/ppermute | solution.py:22
  53.3 6.0 %collective-permute-done.14.refs_1_ = bf16[128,1024]{1,0:T(8,128)(2,1)S(1)} collective-permute-done((bf16[128,1024]{1,0:T(8,128)(2,1)S(1)}, bf16[128,1024]{1,0:T(8,128)(2,1)S(1)}, u32[]{:S(2)}, u32[]{:S(2)}) %collective-permute-start.14) | collective-permute-done | bytes 262176 | tf_op jit(solution)/shard_map/ppermute | solution.py:22
  59.2 5.1 %collective-permute-done.7.came = bf16[128,1024]{1,0:T(8,128)(2,1)S(1)} collective-permute-done((bf16[128,1024]{1,0:T(8,128)(2,1)S(1)}, bf16[128,1024]{1,0:T(8,128)(2,1)S(1)}, u32[]{:S(2)}, u32[]{:S(2)}) %collective-permute-start.7) | collective-permute-done | bytes 262176 | tf_op jit(solution)/shard_map/ppermute | solution.py:22
  64.4 0.2 shard_map.109
  64.6 0.7 shard_map.112
  65.3 2.9 %collective-permute-start.17 = (bf16[128,1024]{1,0:T(8,128)(2,1)S(1)}, bf16[128,1024]{1,0:T(8,128)(2,1)S(1)}, u32[]{:S(2)}, u32[]{:S(2)}) collective-permute-start(bf16[128,1024]{1,0:T(8,128)(2,1)S(1)} %get-tuple-element.48.refs_0_), channel_id=1, source_target_pairs={{0,2},{1,3},{2,0},{3,1},{4,6},{5,7},{6,4},{7,5},{8,10},{9,11},{10,... | collective-permute-start | bytes 786440 | tf_op jit(solution)/shard_map/ppermute | solution.py:22
  68.2 3.7 %collective-permute-start.11 = (bf16[128,1024]{1,0:T(8,128)(2,1)S(1)}, bf16[128,1024]{1,0:T(8,128)(2,1)S(1)}, u32[]{:S(2)}, u32[]{:S(2)}) collective-permute-start(bf16[128,1024]{1,0:T(8,128)(2,1)S(1)} %get-tuple-element.40.refs_5_.hidden), channel_id=1, source_target_pairs={{0,248},{4,252},{8,0},{12,4},{16,8},{20,12},{24,16},{28,20},{32,24... | collective-permute-start | bytes 786440 | tf_op jit(solution)/shard_map/ppermute | solution.py:18
  71.9 2.1 %collective-permute-start.10 = (bf16[128,1024]{1,0:T(8,128)(2,1)S(1)}, bf16[128,1024]{1,0:T(8,128)(2,1)S(1)}, u32[]{:S(2)}, u32[]{:S(2)}) collective-permute-start(bf16[128,1024]{1,0:T(8,128)(2,1)S(1)} %get-tuple-element.40.refs_5_.hidden), channel_id=1, source_target_pairs={{0,252},{4,0},{8,4},{12,8},{16,12},{20,16},{24,20},{28,24},{32,28}... | collective-permute-start | bytes 786440 | tf_op jit(solution)/shard_map/ppermute | solution.py:18
  73.9 1.5 %collective-permute-start.9 = (bf16[128,1024]{1,0:T(8,128)(2,1)S(1)}, bf16[128,1024]{1,0:T(8,128)(2,1)S(1)}, u32[]{:S(2)}, u32[]{:S(2)}) collective-permute-start(bf16[128,1024]{1,0:T(8,128)(2,1)S(1)} %get-tuple-element.40.refs_5_.hidden), channel_id=1, source_target_pairs={{0,4},{4,8},{8,12},{12,16},{16,20},{20,24},{24,28},{28,32},{32,36}... | collective-permute-start | bytes 786440 | tf_op jit(solution)/shard_map/ppermute | solution.py:18
  75.4 1.5 %collective-permute-start.8 = (bf16[128,1024]{1,0:T(8,128)(2,1)S(1)}, bf16[128,1024]{1,0:T(8,128)(2,1)S(1)}, u32[]{:S(2)}, u32[]{:S(2)}) collective-permute-start(bf16[128,1024]{1,0:T(8,128)(2,1)S(1)} %get-tuple-element.40.refs_5_.hidden), channel_id=1, source_target_pairs={{0,8},{4,12},{8,16},{12,20},{16,24},{20,28},{24,32},{28,36},{32,40... | collective-permute-start | bytes 786440 | tf_op jit(solution)/shard_map/ppermute | solution.py:18
  76.9 3.3 %collective-permute-done.11.refs_7_ = bf16[128,1024]{1,0:T(8,128)(2,1)S(1)} collective-permute-done((bf16[128,1024]{1,0:T(8,128)(2,1)S(1)}, bf16[128,1024]{1,0:T(8,128)(2,1)S(1)}, u32[]{:S(2)}, u32[]{:S(2)}) %collective-permute-start.11) | collective-permute-done | bytes 262176 | tf_op jit(solution)/shard_map/ppermute | solution.py:18
  80.2 10.8 %collective-permute-done.10.refs_6_ = bf16[128,1024]{1,0:T(8,128)(2,1)S(1)} collective-permute-done((bf16[128,1024]{1,0:T(8,128)(2,1)S(1)}, bf16[128,1024]{1,0:T(8,128)(2,1)S(1)}, u32[]{:S(2)}, u32[]{:S(2)}) %collective-permute-start.10) | collective-permute-done | bytes 262176 | tf_op jit(solution)/shard_map/ppermute | solution.py:18
  91.0 2.3 %collective-permute-done.8.refs_3_ = bf16[128,1024]{1,0:T(8,128)(2,1)S(1)} collective-permute-done((bf16[128,1024]{1,0:T(8,128)(2,1)S(1)}, bf16[128,1024]{1,0:T(8,128)(2,1)S(1)}, u32[]{:S(2)}, u32[]{:S(2)}) %collective-permute-start.8) | collective-permute-done | bytes 262176 | tf_op jit(solution)/shard_map/ppermute | solution.py:18
  93.3 2.8 %shard_map.110 = (bf16[256,1024]{1,0:T(8,128)(2,1)S(1)}, bf16[256,1024]{1,0:T(8,128)(2,1)S(1)}) custom-call(s32[4,6]{1,0:T(4,128)S(1)} %copy-done.7, s32[4]{0:T(128)S(1)} %copy-done.11, s32[256]{0:T(256)S(1)} %copy-done.9, bf16[128,1024]{1,0:T(8,128)(2,1)S(1)} %collective-permute-done.8.refs_3_, bf16[128,1024]{1,0:T(8,128)(2,1)S(1)} %collective-permute-done.9.refs_4_, ...), custom_call_target="tpu_custom_call" | custom-call | tf_op jit(solution)/shard_map/pallas_call | solution.py:239
  96.1 0.1 collective-permute-start.12
  96.2 0.4 shard_map.113
  96.6 21.2 %all_to_all.22 = bf16[64,16,128]{2,1,0:T(8,128)(2,1)S(1)} all-to-all(bf16[64,16,128]{2,1,0:T(8,128)(2,1)S(1)} %bitcast.6), channel_id=1, replica_groups=mesh['blk'=64,'rep'=4] {'blk'}, dimensions={0} | all-to-all | bytes 524288 | tf_op jit(solution)/shard_map/all_to_all | solution.py:318
  117.8 0.8 shard_map.114
  118.6 4.9 %all-to-all-start.1 = ((bf16[64,16,128]{2,1,0:T(8,128)(2,1)}), bf16[64,16,128]{2,1,0:T(8,128)(2,1)S(1)}, u32[]{:S(2)}, u32[]{:S(2)}) async-start(bf16[64,16,128]{2,1,0:T(8,128)(2,1)} %bitcast.2), calls=%async_computation.1 | async-start | bytes 524288 | tf_op jit(solution)/shard_map/all_to_all | solution.py:320
  123.5 0.1 shard_map.111
  123.6 1.1 collective-permute-start.13
  124.7 9.9 %collective-permute-done.13 = bf16[128,1024]{1,0:T(8,128)(2,1)S(1)} collective-permute-done((bf16[128,1024]{1,0:T(8,128)(2,1)S(1)}, bf16[128,1024]{1,0:T(8,128)(2,1)S(1)}, u32[]{:S(2)}, u32[]{:S(2)}) %collective-permute-start.13) | collective-permute-done | bytes 262176 | tf_op jit(solution)/shard_map/ppermute | solution.py:22
  134.6 0.8 add_convert_fusion
  135.3 0.9 all-to-all-done.1
  136.2 0.8 shard_map.115
  (33 shorter events, 0.1 us)
Async XLA Ops:
  0.6 15.8 %collective-permute-start = (bf16[128,1024]{1,0:T(8,128)(2,1)}, bf16[128,1024]{1,0:T(8,128)(2,1)S(1)}, u32[]{:S(2)}, u32[]{:S(2)}) collective-permute-start(bf16[128,1024]{1,0:T(8,128)(2,1)} %refs_5_.1), channel_id=1, source_target_pairs={{0,4},{4,8},{8,12},{12,16},{16,20},{20,24},{24,28},{28,32},{32,36}... | collective-permute-start | bytes 786440 | tf_op jit(solution)/shard_map/ppermute | solution.py:18
  2.6 13.8 %collective-permute-start.1 = (bf16[128,1024]{1,0:T(8,128)(2,1)}, bf16[128,1024]{1,0:T(8,128)(2,1)S(1)}, u32[]{:S(2)}, u32[]{:S(2)}) collective-permute-start(bf16[128,1024]{1,0:T(8,128)(2,1)} %refs_5_.1), channel_id=1, source_target_pairs={{0,252},{4,0},{8,4},{12,8},{16,12},{20,16},{24,20},{28,24},{32,28}... | collective-permute-start | bytes 786440 | tf_op jit(solution)/shard_map/ppermute | solution.py:18
  8.7 1.9 %copy-start = (bf16[4,6,256,256]{3,2,1,0:T(8,128)(2,1)S(1)}, bf16[4,6,256,256]{3,2,1,0:T(8,128)(2,1)}, u32[]{:S(2)}) copy-start(bf16[4,6,256,256]{3,2,1,0:T(8,128)(2,1)} %refs_8_.3) | copy-start | bytes 9437188
  10.6 0.9 copy-start.3
  11.6 0.7 copy-start.6
  12.3 0.7 copy-start.8
  12.9 0.7 copy-start.10
  13.6 32.0 %copy-start.1 = (bf16[4,6,256,256]{3,2,1,0:T(8,128)(2,1)S(1)}, bf16[4,6,256,256]{3,2,1,0:T(8,128)(2,1)}, u32[]{:S(2)}) copy-start(bf16[4,6,256,256]{3,2,1,0:T(8,128)(2,1)} %refs_8_.3) | copy-start | bytes 9437188
  13.6 32.0 %copy-start.4 = (bf16[128,1024]{1,0:T(8,128)(2,1)S(1)}, bf16[128,1024]{1,0:T(8,128)(2,1)}, u32[]{:S(2)}) copy-start(bf16[128,1024]{1,0:T(8,128)(2,1)} %refs_5_.1) | copy-start | bytes 786436
  13.6 32.0 %copy-start.5 = (bf16[128,512]{1,0:T(8,128)(2,1)S(1)}, bf16[128,512]{1,0:T(8,128)(2,1)}, u32[]{:S(2)}) copy-start(bf16[128,512]{1,0:T(8,128)(2,1)} %refs_9_.2) | copy-start | bytes 393220
  13.6 32.0 %copy-start.7 = (s32[4,6]{1,0:T(4,128)S(1)}, s32[4,6]{1,0:T(4,128)}, u32[]{:S(2)}) copy-start(s32[4,6]{1,0:T(4,128)} %refs_0_.5) | copy-start | bytes 292
  13.6 32.0 %copy-start.9 = (s32[256]{0:T(256)S(1)}, s32[256]{0:T(256)}, u32[]{:S(2)}) copy-start(s32[256]{0:T(256)} %refs_2_.5) | copy-start | bytes 3076
  13.6 32.0 %copy-start.11 = (s32[4]{0:T(128)S(1)}, s32[4]{0:T(128)}, u32[]{:S(2)}) copy-start(s32[4]{0:T(128)} %refs_1_.5) | copy-start | bytes 52
  16.5 17.7 %collective-permute-start.2 = (bf16[256,1024]{1,0:T(8,128)(2,1)S(1)}, bf16[256,1024]{1,0:T(8,128)(2,1)S(1)}, u32[]{:S(2)}, u32[]{:S(2)}) collective-permute-start(bf16[256,1024]{1,0:T(8,128)(2,1)S(1)} %get-tuple-element.32), channel_id=1, source_target_pairs={{0,4},{4,8},{8,12},{12,16},{16,20},{20,24},{24,28},{28,32},{32,36}... | collective-permute-start | bytes 1572872 | tf_op jit(solution)/shard_map/ppermute | solution.py:18
  16.6 17.6 %collective-permute-start.3 = (bf16[256,1024]{1,0:T(8,128)(2,1)S(1)}, bf16[256,1024]{1,0:T(8,128)(2,1)S(1)}, u32[]{:S(2)}, u32[]{:S(2)}) collective-permute-start(bf16[256,1024]{1,0:T(8,128)(2,1)S(1)} %get-tuple-element.33), channel_id=1, source_target_pairs={{0,252},{4,0},{8,4},{12,8},{16,12},{20,16},{24,20},{28,24},{32,28}... | collective-permute-start | bytes 1572872 | tf_op jit(solution)/shard_map/ppermute | solution.py:18
  34.3 11.1 %collective-permute-start.4 = (bf16[128,1024]{1,0:T(8,128)(2,1)S(1)}, bf16[128,1024]{1,0:T(8,128)(2,1)S(1)}, u32[]{:S(2)}, u32[]{:S(2)}) collective-permute-start(bf16[128,1024]{1,0:T(8,128)(2,1)S(1)} %get-tuple-element.34), channel_id=1, source_target_pairs={{0,4},{4,8},{8,12},{12,16},{16,20},{20,24},{24,28},{28,32},{32,36}... | collective-permute-start | bytes 786440 | tf_op jit(solution)/shard_map/ppermute | solution.py:18
  34.4 11.1 %collective-permute-start.5 = (bf16[128,1024]{1,0:T(8,128)(2,1)S(1)}, bf16[128,1024]{1,0:T(8,128)(2,1)S(1)}, u32[]{:S(2)}, u32[]{:S(2)}) collective-permute-start(bf16[128,1024]{1,0:T(8,128)(2,1)S(1)} %get-tuple-element.35), channel_id=1, source_target_pairs={{0,252},{4,0},{8,4},{12,8},{16,12},{20,16},{24,20},{28,24},{32,28}... | collective-permute-start | bytes 786440 | tf_op jit(solution)/shard_map/ppermute | solution.py:18
  45.7 19.0 %copy-start.2 = (bf16[128,512]{1,0:T(8,128)(2,1)S(1)}, bf16[128,512]{1,0:T(8,128)(2,1)}, u32[]{:S(2)}) copy-start(bf16[128,512]{1,0:T(8,128)(2,1)} %weight.1) | copy-start | bytes 393220
  48.4 2.8 %collective-permute-start.6 = (bf16[256,1024]{1,0:T(8,128)(2,1)S(1)}, bf16[256,1024]{1,0:T(8,128)(2,1)S(1)}, u32[]{:S(2)}, u32[]{:S(2)}) collective-permute-start(bf16[256,1024]{1,0:T(8,128)(2,1)S(1)} %get-tuple-element.37), channel_id=1, source_target_pairs={{0,1},{1,0},{2,3},{3,2},{4,5},{5,4},{6,7},{7,6},{8,9},{9,8},{10,11... | collective-permute-start | bytes 1572872 | tf_op jit(solution)/shard_map/ppermute | solution.py:22
  48.5 10.7 %collective-permute-start.14 = (bf16[128,1024]{1,0:T(8,128)(2,1)S(1)}, bf16[128,1024]{1,0:T(8,128)(2,1)S(1)}, u32[]{:S(2)}, u32[]{:S(2)}) collective-permute-start(bf16[128,1024]{1,0:T(8,128)(2,1)S(1)} %shard_map.106._.refs_0_), channel_id=1, source_target_pairs={{0,2},{1,3},{2,0},{3,1},{4,6},{5,7},{6,4},{7,5},{8,10},{9,11},{10,... | collective-permute-start | bytes 786440 | tf_op jit(solution)/shard_map/ppermute | solution.py:22
  51.4 13.0 %collective-permute-start.7 = (bf16[128,1024]{1,0:T(8,128)(2,1)S(1)}, bf16[128,1024]{1,0:T(8,128)(2,1)S(1)}, u32[]{:S(2)}, u32[]{:S(2)}) collective-permute-start(bf16[128,1024]{1,0:T(8,128)(2,1)S(1)} %get-tuple-element.39), channel_id=1, source_target_pairs={{0,2},{1,3},{2,0},{3,1},{4,6},{5,7},{6,4},{7,5},{8,10},{9,11},{10,... | collective-permute-start | bytes 786440 | tf_op jit(solution)/shard_map/ppermute | solution.py:22
  53.3 11.3 %collective-permute-start.15 = (bf16[128,1024]{1,0:T(8,128)(2,1)S(1)}, bf16[128,1024]{1,0:T(8,128)(2,1)S(1)}, u32[]{:S(2)}, u32[]{:S(2)}) collective-permute-start(bf16[128,1024]{1,0:T(8,128)(2,1)S(1)} %shard_map.106._.refs_0_), channel_id=1, source_target_pairs={{0,1},{1,0},{2,3},{3,2},{4,5},{5,4},{6,7},{7,6},{8,9},{9,8},{10,11... | collective-permute-start | bytes 786440 | tf_op jit(solution)/shard_map/ppermute | solution.py:22
  59.2 5.4 %collective-permute-start.16 = (bf16[128,1024]{1,0:T(8,128)(2,1)S(1)}, bf16[128,1024]{1,0:T(8,128)(2,1)S(1)}, u32[]{:S(2)}, u32[]{:S(2)}) collective-permute-start(bf16[128,1024]{1,0:T(8,128)(2,1)S(1)} %collective-permute-done.14.refs_1_), channel_id=1, source_target_pairs={{0,1},{1,0},{2,3},{3,2},{4,5},{5,4},{6,7},{7,6},{8,9},{9,8},{10,11... | collective-permute-start | bytes 786440 | tf_op jit(solution)/shard_map/ppermute | solution.py:22
  65.3 11.5 %collective-permute-start.17 = (bf16[128,1024]{1,0:T(8,128)(2,1)S(1)}, bf16[128,1024]{1,0:T(8,128)(2,1)S(1)}, u32[]{:S(2)}, u32[]{:S(2)}) collective-permute-start(bf16[128,1024]{1,0:T(8,128)(2,1)S(1)} %get-tuple-element.48.refs_0_), channel_id=1, source_target_pairs={{0,2},{1,3},{2,0},{3,1},{4,6},{5,7},{6,4},{7,5},{8,10},{9,11},{10,... | collective-permute-start | bytes 786440 | tf_op jit(solution)/shard_map/ppermute | solution.py:22
  68.2 12.0 %collective-permute-start.11 = (bf16[128,1024]{1,0:T(8,128)(2,1)S(1)}, bf16[128,1024]{1,0:T(8,128)(2,1)S(1)}, u32[]{:S(2)}, u32[]{:S(2)}) collective-permute-start(bf16[128,1024]{1,0:T(8,128)(2,1)S(1)} %get-tuple-element.40.refs_5_.hidden), channel_id=1, source_target_pairs={{0,248},{4,252},{8,0},{12,4},{16,8},{20,12},{24,16},{28,20},{32,24... | collective-permute-start | bytes 786440 | tf_op jit(solution)/shard_map/ppermute | solution.py:18
  71.9 19.2 %collective-permute-start.10 = (bf16[128,1024]{1,0:T(8,128)(2,1)S(1)}, bf16[128,1024]{1,0:T(8,128)(2,1)S(1)}, u32[]{:S(2)}, u32[]{:S(2)}) collective-permute-start(bf16[128,1024]{1,0:T(8,128)(2,1)S(1)} %get-tuple-element.40.refs_5_.hidden), channel_id=1, source_target_pairs={{0,252},{4,0},{8,4},{12,8},{16,12},{20,16},{24,20},{28,24},{32,28}... | collective-permute-start | bytes 786440 | tf_op jit(solution)/shard_map/ppermute | solution.py:18
  73.9 17.1 %collective-permute-start.9 = (bf16[128,1024]{1,0:T(8,128)(2,1)S(1)}, bf16[128,1024]{1,0:T(8,128)(2,1)S(1)}, u32[]{:S(2)}, u32[]{:S(2)}) collective-permute-start(bf16[128,1024]{1,0:T(8,128)(2,1)S(1)} %get-tuple-element.40.refs_5_.hidden), channel_id=1, source_target_pairs={{0,4},{4,8},{8,12},{12,16},{16,20},{20,24},{24,28},{28,32},{32,36}... | collective-permute-start | bytes 786440 | tf_op jit(solution)/shard_map/ppermute | solution.py:18
  75.4 17.9 %collective-permute-start.8 = (bf16[128,1024]{1,0:T(8,128)(2,1)S(1)}, bf16[128,1024]{1,0:T(8,128)(2,1)S(1)}, u32[]{:S(2)}, u32[]{:S(2)}) collective-permute-start(bf16[128,1024]{1,0:T(8,128)(2,1)S(1)} %get-tuple-element.40.refs_5_.hidden), channel_id=1, source_target_pairs={{0,8},{4,12},{8,16},{12,20},{16,24},{20,28},{24,32},{28,36},{32,40... | collective-permute-start | bytes 786440 | tf_op jit(solution)/shard_map/ppermute | solution.py:18
  76.9 19.3 %collective-permute-start.18 = (bf16[128,1024]{1,0:T(8,128)(2,1)S(1)}, bf16[128,1024]{1,0:T(8,128)(2,1)S(1)}, u32[]{:S(2)}, u32[]{:S(2)}) collective-permute-start(bf16[128,1024]{1,0:T(8,128)(2,1)S(1)} %get-tuple-element.48.refs_0_), channel_id=1, source_target_pairs={{0,1},{1,0},{2,3},{3,2},{4,5},{5,4},{6,7},{7,6},{8,9},{9,8},{10,11... | collective-permute-start | bytes 786440 | tf_op jit(solution)/shard_map/ppermute | solution.py:22
  80.2 16.0 %collective-permute-start.19 = (bf16[128,1024]{1,0:T(8,128)(2,1)S(1)}, bf16[128,1024]{1,0:T(8,128)(2,1)S(1)}, u32[]{:S(2)}, u32[]{:S(2)}) collective-permute-start(bf16[128,1024]{1,0:T(8,128)(2,1)S(1)} %collective-permute-done.17.refs_1_), channel_id=1, source_target_pairs={{0,1},{1,0},{2,3},{3,2},{4,5},{5,4},{6,7},{7,6},{8,9},{9,8},{10,11... | collective-permute-start | bytes 786440 | tf_op jit(solution)/shard_map/ppermute | solution.py:22
  96.1 27.4 %collective-permute-start.12 = (bf16[256,1024]{1,0:T(8,128)(2,1)S(1)}, bf16[256,1024]{1,0:T(8,128)(2,1)S(1)}, u32[]{:S(2)}, u32[]{:S(2)}) collective-permute-start(bf16[256,1024]{1,0:T(8,128)(2,1)S(1)} %get-tuple-element.42), channel_id=1, source_target_pairs={{0,1},{1,0},{2,3},{3,2},{4,5},{5,4},{6,7},{7,6},{8,9},{9,8},{10,11... | collective-permute-start | bytes 1572872 | tf_op jit(solution)/shard_map/ppermute | solution.py:22
  118.6 17.6 %all-to-all-start.1 = ((bf16[64,16,128]{2,1,0:T(8,128)(2,1)}), bf16[64,16,128]{2,1,0:T(8,128)(2,1)S(1)}, u32[]{:S(2)}, u32[]{:S(2)}) async-start(bf16[64,16,128]{2,1,0:T(8,128)(2,1)} %bitcast.2), calls=%async_computation.1 | async-start | bytes 524288 | tf_op jit(solution)/shard_map/all_to_all | solution.py:320
  123.6 11.0 %collective-permute-start.13 = (bf16[128,1024]{1,0:T(8,128)(2,1)S(1)}, bf16[128,1024]{1,0:T(8,128)(2,1)S(1)}, u32[]{:S(2)}, u32[]{:S(2)}) collective-permute-start(bf16[128,1024]{1,0:T(8,128)(2,1)S(1)} %get-tuple-element.44), channel_id=1, source_target_pairs={{0,2},{1,3},{2,0},{3,1},{4,6},{5,7},{6,4},{7,5},{8,10},{9,11},{10,... | collective-permute-start | bytes 786440 | tf_op jit(solution)/shard_map/ppermute | solution.py:22

commit v3 on v2

--- a/solution.py
+++ b/solution.py
@@ -9,13 +9,19 @@
 BF16 = jnp.bfloat16
 REACH = 2
 SIDES = 2 * REACH + 1
-FAR_FIRST = (0, 4, 1, 3)
 FLIPS = (0, 2, 1, 3)
 
 
-def behind(array, by):
+def swap(array, step, turn):
     peers = lax.axis_size("blk")
-    return lax.ppermute(array, "blk", [(i, (i + by) % peers) for i in range(peers)])
+    shift = step * turn
+    return lax.ppermute(array, "blk", [(i, (((i + shift) ^ step) - shift) % peers) for i in range(peers)])
+
+
+def sides_of(here, step):
+    upward = lax.rem(here // step, 2) == 0
+    first = jnp.where(upward, REACH + step, REACH - step)
+    return first, 2 * REACH - first
 
 
 def across(array, flip):
@@ -76,18 +82,19 @@
         rows_out[:, row * block : (row + 1) * block] = (total[row] * inverse_root(degree)).astype(BF16)
 
 
-def join_kernel(ahead, back, part_ahead, part_back, join_ahead, join_back):
-    width = ahead.shape[0]
-    join_ahead[:width] = ahead[...]
-    join_ahead[width:] = part_ahead[...]
-    join_back[:width] = back[...]
-    join_back[width:] = part_back[...]
-
-
-def relay_kernel(part_ahead, part_back, far_ahead, far_back, sum_ahead, sum_back):
-    width = sum_ahead.shape[0]
-    sum_ahead[...] = (part_ahead[...].astype(F32) + far_ahead[width:].astype(F32)).astype(BF16)
-    sum_back[...] = (part_back[...].astype(F32) + far_back[width:].astype(F32)).astype(BF16)
+def join_kernel(*refs):
+    arrived, parts, joined = refs[:2], refs[2:4], refs[4:]
+    width = arrived[0].shape[0]
+    for turn in range(2):
+        joined[turn][:width] = arrived[1 - turn][...]
+        joined[turn][width:] = parts[turn][...]
+
+
+def relay_kernel(*refs):
+    parts, arrived, sums = refs[:2], refs[2:4], refs[4:]
+    width = sums[0].shape[0]
+    for turn in range(2):
+        sums[turn][...] = (parts[turn][...].astype(F32) + arrived[1 - turn][width:].astype(F32)).astype(BF16)
 
 
 def add_kernel(part, came_ahead, came_back, spread):
@@ -95,14 +102,22 @@
     spread[...] = total.astype(BF16)
 
 
+def hold(held, own, pieces, blocks, block, far):
+    here = lax.axis_index("blk")
+    width = own.shape[0]
+    ups = sides_of(here, 1)
+    twos = (2 * ups[0] - REACH, 2 * ups[1] - REACH) if far else sides_of(here, 2)
+    for side, ref in zip((REACH, *ups, *twos), (own, *pieces)):
+        for inner in range(blocks):
+            held[side * blocks + inner] = ref[:width, inner * block : (inner + 1) * block]
+
+
 def first_kernel(peers, slot_blocks, degrees, block_position, *refs):
-    far_ahead, near_ahead, own, near_back, far_back = refs[:5]
+    own, pieces = refs[0], refs[1:5]
     tiles, weight, rows_out, keep_out, send_out, held, total = refs[5:]
     blocks, _, block, _ = tiles.shape
     width = own.shape[0]
-    for side, ref in enumerate((far_ahead, near_ahead, own, near_back, far_back)):
-        for inner in range(blocks):
-            held[side * blocks + inner] = ref[:width, inner * block : (inner + 1) * block]
+    hold(held, own, pieces, blocks, block, far=True)
     gather_rows(peers, slot_blocks, degrees, block_position, tiles, held, total, rows_out)
     mix_rows(lax.axis_index("rep"), weight, rows_out[...], keep_out, send_out)
 
@@ -110,9 +125,7 @@
 def second_kernel(peers, slot_blocks, degrees, block_position, *refs):
     held_refs, (tiles, weight, keep_out, send_out, held, total, rows) = refs[:SIDES], refs[SIDES:]
     blocks, _, block, _ = tiles.shape
-    for side in range(SIDES):
-        for inner in range(blocks):
-            held[side * blocks + inner] = held_refs[side][:, inner * block : (inner + 1) * block]
+    hold(held, held_refs[0], held_refs[1:], blocks, block, far=False)
     gather_rows(peers, slot_blocks, degrees, block_position, tiles, held, total, rows)
     mix_rows(lax.axis_index("rep"), weight, rows[...], keep_out, send_out)
 
@@ -141,9 +154,11 @@
                 add()
             else:
                 pl.when(slot < degree)(add)
-    for side in range(SIDES):
+    ups = sides_of(here, 1)
+    sides = (REACH, *ups, 2 * ups[0] - REACH, 2 * ups[1] - REACH)
+    for side, out in zip(sides, outs):
         for inner in range(blocks):
-            outs[side][:, inner * block : (inner + 1) * block] = total[side * blocks + inner].astype(BF16)
+            out[:, inner * block : (inner + 1) * block] = total[side * blocks + inner].astype(BF16)
 
 
 def settle_kernel(keep, came, mine, other):
@@ -247,17 +262,11 @@
             cost_estimate=pl.CostEstimate(flops=0, bytes_accessed=0, transcendentals=0),
         )(*args)
 
-    def halo(values):
-        held = {side: behind(values, REACH - side) for side in FAR_FIRST}
-        held[REACH] = values
-        return [held[side] for side in range(SIDES)]
-
     def gather(own, far):
         return own, far, across(own, 1), across(far, 1)
 
     pair = jax.ShapeDtypeStruct((2 * width, node_local), BF16)
-    near_ahead = behind(node_features, 1)
-    near_back = behind(node_features, -1)
+    near = [swap(node_features, 1, turn) for turn in range(2)]
     parts = call(
         lambda *refs: spread_kernel(peers, *refs),
         (node,) * SIDES,
@@ -273,26 +282,24 @@
             pltpu.SemaphoreType.DMA((blocks,)),
         ],
     )
-    joined = call(join_kernel, (pair, pair), [VMEM] * 4, near_ahead, near_back, parts[4], parts[0])
-    far_ahead, far_back = behind(joined[0], 1), behind(joined[1], -1)
-    sums = call(relay_kernel, (node, node), [VMEM] * 4, parts[3], parts[1], far_ahead, far_back)
-    came_ahead, came_back = behind(sums[0], 1), behind(sums[1], -1)
+    joined = call(join_kernel, (pair, pair), [VMEM] * 4, *near, *parts[3:])
+    far = [swap(joined[turn], 1, turn) for turn in range(2)]
+    sums = call(relay_kernel, (node, node), [VMEM] * 4, *parts[1:3], *far)
+    came_parts = [swap(sums[turn], 1, turn) for turn in range(2)]
     held_scratch = [
         pltpu.VMEM((SIDES * blocks, width, block), BF16),
         pltpu.VMEM((blocks, width, block), F32),
     ]
-    spread = call(add_kernel, node, [VMEM] * 3, parts[REACH], came_ahead, came_back)
+    spread = call(add_kernel, node, [VMEM] * 3, parts[0], *came_parts)
     ax_rows, keep, send = call(
         lambda _, *refs: first_kernel(peers, *refs),
         (node, half, half),
         [ANY] + [SMEM] * 3 + [VMEM] * 7,
         spread,
         *lists,
-        far_ahead,
-        near_ahead,
         node_features,
-        near_back,
-        far_back,
+        *near,
+        *far,
         tiles,
         weight_first,
         scratch=held_scratch,
@@ -302,7 +309,7 @@
     came = across(other, 2)
     spread_all = gather(spread, across(spread, 2))
     hidden, slope = call(activate_kernel, (node, node_wide), [VMEM] * 2, mine, came)
-    held_h = halo(hidden)
+    held_h = (hidden, *(swap(hidden, step, turn) for step in (1, 2) for turn in range(2)))
     hidden_grad, term_second = call(
         back_kernel,
         (node, jax.ShapeDtypeStruct((full, full // 4), BF16)),

time: 137 us -> 134 us (0.978)
  starting transfers between devices: 43 us -> 34.3 us
  waiting for transfers between devices: 54.4 us -> 58.6 us
    ppermute x10, starting transfers between devices: 29.4 us -> 21.9 us  [swap(): lax.ppermute(array, 'blk', [(i, ((i + shift ^ step) - shift) % peers) for...]
    ppermute x10, waiting for transfers between devices: 21 us -> 24 us  [across(): lax.ppermute(array, 'rep', [(i, i ^ flip) for i in range(lax.axis_size('r...]
  transfers between devices with their start and end apart: 21 -> 21, of which waited for: 9 -> 11; matrix products, arithmetic and copies ran while one was open for 1% -> 1% of each run, Pallas kernels for 5% -> 6%
where the time goes in v3:
time: 134 us
  waiting for transfers between devices  58.6 us (44%)
  starting transfers between devices  34.3 us (26%)
  blocking collectives  21.8 us (16%)
  Pallas kernels  12.4 us (9%)
  local copies, waits for them, and re-layouts  4.88 us (4%)
    ppermute x10, waiting for transfers between devices, swap(): lax.ppermute(array, 'blk', [(i, ((i + shift ^ step) - shift) % peers) for...  33.5 us
    ppermute x10, waiting for transfers between devices, across(): lax.ppermute(array, 'rep', [(i, i ^ flip) for i in range(lax.axis_size('r...  24 us
    ppermute x10, starting transfers between devices, swap(): lax.ppermute(array, 'blk', [(i, ((i + shift ^ step) - shift) % peers) for...  21.9 us
    all_to_all x1, blocking collectives, body(): got = lax.all_to_all(terms, 'blk', 0, 0, tiled=True)  21.8 us
    pallas_call x13, Pallas kernels, call(): pl.pallas_call(kernel, out_shape=outs, in_specs=in_specs, out_specs=out_s...  12.4 us
    ppermute x10, starting transfers between devices, across(): lax.ppermute(array, 'rep', [(i, i ^ flip) for i in range(lax.axis_size('r...  7.53 us
    unnamed x24, local copies, waits for them, and re-layouts  4.88 us
    all_to_all x1, starting transfers between devices, body(): everyone = lax.all_to_all(chunks, 'blk', 0, 0, tiled=True)  4.88 us
  transfers between devices with their start and end apart: 21, of which 11 were waited for; matrix products, arithmetic and copies ran while one was open for 1% of the time, Pallas kernels for 6%

profile of v3, /device:TPU:8, one launch (start us, length us, event | category | flops | bytes accessed | tf_op | source)
XLA Modules:
  0.0 133.7 jit_solution(3303677106148886232)
XLA Ops:
  0.6 2.0 %collective-permute-start = (bf16[128,1024]{1,0:T(8,128)(2,1)}, bf16[128,1024]{1,0:T(8,128)(2,1)S(1)}, u32[]{:S(2)}, u32[]{:S(2)}) collective-permute-start(bf16[128,1024]{1,0:T(8,128)(2,1)} %refs_3_.3), channel_id=1, source_target_pairs={{0,4},{4,0},{8,12},{12,8},{16,20},{20,16},{24,28},{28,24},{32,36},... | collective-permute-start | bytes 786440 | tf_op jit(solution)/shard_map/ppermute | solution.py:18
  2.6 7.0 %collective-permute-start.1 = (bf16[128,1024]{1,0:T(8,128)(2,1)}, bf16[128,1024]{1,0:T(8,128)(2,1)S(1)}, u32[]{:S(2)}, u32[]{:S(2)}) collective-permute-start(bf16[128,1024]{1,0:T(8,128)(2,1)} %refs_3_.3), channel_id=1, source_target_pairs={{0,252},{4,8},{8,4},{12,16},{16,12},{20,24},{24,20},{28,32},{32,28... | collective-permute-start | bytes 786440 | tf_op jit(solution)/shard_map/ppermute | solution.py:18
  9.7 1.9 %copy-done = bf16[4,6,256,256]{3,2,1,0:T(8,128)(2,1)S(1)} copy-done((bf16[4,6,256,256]{3,2,1,0:T(8,128)(2,1)S(1)}, bf16[4,6,256,256]{3,2,1,0:T(8,128)(2,1)}, u32[]{:S(2)}) %copy-start) | copy-done | bytes 3145752
  11.6 0.9 copy-done.3
  12.5 0.7 copy-done.6
  13.2 0.7 copy-done.8
  13.9 0.7 copy-done.10
  14.6 3.0 %shard_map.103 = (bf16[128,1024]{1,0:T(8,128)(2,1)S(1)}, bf16[128,1024]{1,0:T(8,128)(2,1)S(1)}, bf16[128,1024]{1,0:T(8,128)(2,1)S(1)}, bf16[128,1024]{1,0:T(8,128)(2,1)S(1)}, bf16[128,1024]{1,0:T(8,128)(2,1)S(1)}) custom-call(s32[4,6]{1,0:T(4,128)S(1)} %copy-done.6, s32[4]{0:T(128)S(1)} %copy-done.10, s32[256]{0:T(256)S(1)} %copy-done.8, ...), custom_call_target="tpu_custom_call" | custom-call | tf_op jit(solution)/shard_map/pallas_call | solution.py:254
  17.6 0.1 shard_map.104
  17.6 0.1 collective-permute-start.2
  17.7 4.4 %collective-permute-start.3 = (bf16[256,1024]{1,0:T(8,128)(2,1)S(1)}, bf16[256,1024]{1,0:T(8,128)(2,1)S(1)}, u32[]{:S(2)}, u32[]{:S(2)}) collective-permute-start(bf16[256,1024]{1,0:T(8,128)(2,1)S(1)} %get-tuple-element.33), channel_id=1, source_target_pairs={{0,252},{4,8},{8,4},{12,16},{16,12},{20,24},{24,20},{28,32},{32,28... | collective-permute-start | bytes 1572872 | tf_op jit(solution)/shard_map/ppermute | solution.py:18
  22.1 8.7 %collective-permute-done.2.refs_2_.refs_6_ = bf16[256,1024]{1,0:T(8,128)(2,1)S(1)} collective-permute-done((bf16[256,1024]{1,0:T(8,128)(2,1)S(1)}, bf16[256,1024]{1,0:T(8,128)(2,1)S(1)}, u32[]{:S(2)}, u32[]{:S(2)}) %collective-permute-start.2) | collective-permute-done | bytes 524320 | tf_op jit(solution)/shard_map/ppermute | solution.py:18
  30.8 4.3 %collective-permute-done.3.refs_3_.refs_7_ = bf16[256,1024]{1,0:T(8,128)(2,1)S(1)} collective-permute-done((bf16[256,1024]{1,0:T(8,128)(2,1)S(1)}, bf16[256,1024]{1,0:T(8,128)(2,1)S(1)}, u32[]{:S(2)}, u32[]{:S(2)}) %collective-permute-start.3) | collective-permute-done | bytes 524320 | tf_op jit(solution)/shard_map/ppermute | solution.py:18
  35.1 0.1 shard_map.105
  35.3 0.1 collective-permute-start.4
  35.4 3.8 %collective-permute-start.5 = (bf16[128,1024]{1,0:T(8,128)(2,1)S(1)}, bf16[128,1024]{1,0:T(8,128)(2,1)S(1)}, u32[]{:S(2)}, u32[]{:S(2)}) collective-permute-start(bf16[128,1024]{1,0:T(8,128)(2,1)S(1)} %get-tuple-element.35), channel_id=1, source_target_pairs={{0,252},{4,8},{8,4},{12,16},{16,12},{20,24},{24,20},{28,32},{32,28... | collective-permute-start | bytes 786440 | tf_op jit(solution)/shard_map/ppermute | solution.py:18
  39.1 2.8 %collective-permute-done.4.came_ahead = bf16[128,1024]{1,0:T(8,128)(2,1)S(1)} collective-permute-done((bf16[128,1024]{1,0:T(8,128)(2,1)S(1)}, bf16[128,1024]{1,0:T(8,128)(2,1)S(1)}, u32[]{:S(2)}, u32[]{:S(2)}) %collective-permute-start.4) | collective-permute-done | bytes 262176 | tf_op jit(solution)/shard_map/ppermute | solution.py:18
  41.9 4.3 %collective-permute-done.5.came_back = bf16[128,1024]{1,0:T(8,128)(2,1)S(1)} collective-permute-done((bf16[128,1024]{1,0:T(8,128)(2,1)S(1)}, bf16[128,1024]{1,0:T(8,128)(2,1)S(1)}, u32[]{:S(2)}, u32[]{:S(2)}) %collective-permute-start.5) | collective-permute-done | bytes 262176 | tf_op jit(solution)/shard_map/ppermute | solution.py:18
  46.2 0.1 shard_map.106._.refs_0_
  46.4 0.0 copy-start.2
  46.4 3.0 %shard_map.107 = (bf16[128,1024]{1,0:T(8,128)(2,1)S(1)}, bf16[256,1024]{1,0:T(8,128)(2,1)S(1)}, bf16[256,1024]{1,0:T(8,128)(2,1)S(1)}) custom-call(bf16[128,1024]{1,0:T(8,128)(2,1)S(1)} %shard_map.106._.refs_0_, s32[4,6]{1,0:T(4,128)S(1)} %copy-done.7, s32[4]{0:T(128)S(1)} %copy-done.11, s32[256]{0:T(256)S(1)} %copy-done.9, bf16[128,1024]{1,0:T(8,128)(2,1)S(1)} %copy-done.4, ...), custom_call_target="tpu_custom_call" | custom-call | tf_op jit(solution)/shard_map/pallas_call | solution.py:254
  49.4 0.1 collective-permute-start.6
  49.5 2.7 %collective-permute-start.14 = (bf16[128,1024]{1,0:T(8,128)(2,1)S(1)}, bf16[128,1024]{1,0:T(8,128)(2,1)S(1)}, u32[]{:S(2)}, u32[]{:S(2)}) collective-permute-start(bf16[128,1024]{1,0:T(8,128)(2,1)S(1)} %shard_map.106._.refs_0_), channel_id=1, source_target_pairs={{0,2},{1,3},{2,0},{3,1},{4,6},{5,7},{6,4},{7,5},{8,10},{9,11},{10,... | collective-permute-start | bytes 786440 | tf_op jit(solution)/shard_map/ppermute | solution.py:28
  52.2 0.1 shard_map.108
  52.3 1.9 %collective-permute-start.7 = (bf16[128,1024]{1,0:T(8,128)(2,1)S(1)}, bf16[128,1024]{1,0:T(8,128)(2,1)S(1)}, u32[]{:S(2)}, u32[]{:S(2)}) collective-permute-start(bf16[128,1024]{1,0:T(8,128)(2,1)S(1)} %get-tuple-element.39), channel_id=1, source_target_pairs={{0,2},{1,3},{2,0},{3,1},{4,6},{5,7},{6,4},{7,5},{8,10},{9,11},{10,... | collective-permute-start | bytes 786440 | tf_op jit(solution)/shard_map/ppermute | solution.py:28
  54.2 6.0 %collective-permute-done.14.refs_1_ = bf16[128,1024]{1,0:T(8,128)(2,1)S(1)} collective-permute-done((bf16[128,1024]{1,0:T(8,128)(2,1)S(1)}, bf16[128,1024]{1,0:T(8,128)(2,1)S(1)}, u32[]{:S(2)}, u32[]{:S(2)}) %collective-permute-start.14) | collective-permute-done | bytes 262176 | tf_op jit(solution)/shard_map/ppermute | solution.py:28
  60.2 5.1 %collective-permute-done.7.came = bf16[128,1024]{1,0:T(8,128)(2,1)S(1)} collective-permute-done((bf16[128,1024]{1,0:T(8,128)(2,1)S(1)}, bf16[128,1024]{1,0:T(8,128)(2,1)S(1)}, u32[]{:S(2)}, u32[]{:S(2)}) %collective-permute-start.7) | collective-permute-done | bytes 262176 | tf_op jit(solution)/shard_map/ppermute | solution.py:28
  65.3 0.2 shard_map.109
  65.6 0.7 shard_map.112
  66.3 2.7 %collective-permute-start.17 = (bf16[128,1024]{1,0:T(8,128)(2,1)S(1)}, bf16[128,1024]{1,0:T(8,128)(2,1)S(1)}, u32[]{:S(2)}, u32[]{:S(2)}) collective-permute-start(bf16[128,1024]{1,0:T(8,128)(2,1)S(1)} %get-tuple-element.48.refs_0_), channel_id=1, source_target_pairs={{0,2},{1,3},{2,0},{3,1},{4,6},{5,7},{6,4},{7,5},{8,10},{9,11},{10,... | collective-permute-start | bytes 786440 | tf_op jit(solution)/shard_map/ppermute | solution.py:28
  69.0 0.2 collective-permute-start.11
  69.2 2.9 %collective-permute-start.9 = (bf16[128,1024]{1,0:T(8,128)(2,1)S(1)}, bf16[128,1024]{1,0:T(8,128)(2,1)S(1)}, u32[]{:S(2)}, u32[]{:S(2)}) collective-permute-start(bf16[128,1024]{1,0:T(8,128)(2,1)S(1)} %get-tuple-element.40.refs_3_.hidden), channel_id=1, source_target_pairs={{0,252},{4,8},{8,4},{12,16},{16,12},{20,24},{24,20},{28,32},{32,28... | collective-permute-start | bytes 786440 | tf_op jit(solution)/shard_map/ppermute | solution.py:18
  72.0 1.5 %collective-permute-start.8 = (bf16[128,1024]{1,0:T(8,128)(2,1)S(1)}, bf16[128,1024]{1,0:T(8,128)(2,1)S(1)}, u32[]{:S(2)}, u32[]{:S(2)}) collective-permute-start(bf16[128,1024]{1,0:T(8,128)(2,1)S(1)} %get-tuple-element.40.refs_3_.hidden), channel_id=1, source_target_pairs={{0,4},{4,0},{8,12},{12,8},{16,20},{20,16},{24,28},{28,24},{32,36},... | collective-permute-start | bytes 786440 | tf_op jit(solution)/shard_map/ppermute | solution.py:18
  73.5 2.3 %collective-permute-done.17.refs_1_ = bf16[128,1024]{1,0:T(8,128)(2,1)S(1)} collective-permute-done((bf16[128,1024]{1,0:T(8,128)(2,1)S(1)}, bf16[128,1024]{1,0:T(8,128)(2,1)S(1)}, u32[]{:S(2)}, u32[]{:S(2)}) %collective-permute-start.17) | collective-permute-done | bytes 262176 | tf_op jit(solution)/shard_map/ppermute | solution.py:28
  75.8 9.9 %collective-permute-done.11.refs_7_ = bf16[128,1024]{1,0:T(8,128)(2,1)S(1)} collective-permute-done((bf16[128,1024]{1,0:T(8,128)(2,1)S(1)}, bf16[128,1024]{1,0:T(8,128)(2,1)S(1)}, u32[]{:S(2)}, u32[]{:S(2)}) %collective-permute-start.11) | collective-permute-done | bytes 262176 | tf_op jit(solution)/shard_map/ppermute | solution.py:18
  85.6 3.5 %collective-permute-done.9.refs_5_ = bf16[128,1024]{1,0:T(8,128)(2,1)S(1)} collective-permute-done((bf16[128,1024]{1,0:T(8,128)(2,1)S(1)}, bf16[128,1024]{1,0:T(8,128)(2,1)S(1)}, u32[]{:S(2)}, u32[]{:S(2)}) %collective-permute-start.9) | collective-permute-done | bytes 262176 | tf_op jit(solution)/shard_map/ppermute | solution.py:18
  89.1 3.0 %shard_map.110 = (bf16[256,1024]{1,0:T(8,128)(2,1)S(1)}, bf16[256,1024]{1,0:T(8,128)(2,1)S(1)}) custom-call(s32[4,6]{1,0:T(4,128)S(1)} %copy-done.7, s32[4]{0:T(128)S(1)} %copy-done.11, s32[256]{0:T(256)S(1)} %copy-done.9, bf16[128,1024]{1,0:T(8,128)(2,1)S(1)} %get-tuple-element.40.refs_3_.hidden, bf16[128,1024]{1,0:T(8,128)(2,1)S(1)} %collective-permute-done.8.refs_4_, ...), custom_call_target="tpu_custom_call" | custom-call | tf_op jit(solution)/shard_map/pallas_call | solution.py:254
  92.1 0.1 collective-permute-start.12
  92.2 0.4 shard_map.113
  92.6 21.8 %all_to_all.22 = bf16[64,16,128]{2,1,0:T(8,128)(2,1)S(1)} all-to-all(bf16[64,16,128]{2,1,0:T(8,128)(2,1)S(1)} %bitcast.6), channel_id=1, replica_groups=mesh['blk'=64,'rep'=4] {'blk'}, dimensions={0} | all-to-all | bytes 524288 | tf_op jit(solution)/shard_map/all_to_all | solution.py:325
  114.4 0.8 shard_map.114
  115.2 4.9 %all-to-all-start.1 = ((bf16[64,16,128]{2,1,0:T(8,128)(2,1)}), bf16[64,16,128]{2,1,0:T(8,128)(2,1)S(1)}, u32[]{:S(2)}, u32[]{:S(2)}) async-start(bf16[64,16,128]{2,1,0:T(8,128)(2,1)} %bitcast.2), calls=%async_computation.1 | async-start | bytes 524288 | tf_op jit(solution)/shard_map/all_to_all | solution.py:327
  120.1 0.1 shard_map.111
  120.2 0.1 collective-permute-start.13
  120.3 10.5 %collective-permute-done.13 = bf16[128,1024]{1,0:T(8,128)(2,1)S(1)} collective-permute-done((bf16[128,1024]{1,0:T(8,128)(2,1)S(1)}, bf16[128,1024]{1,0:T(8,128)(2,1)S(1)}, u32[]{:S(2)}, u32[]{:S(2)}) %collective-permute-start.13) | collective-permute-done | bytes 262176 | tf_op jit(solution)/shard_map/ppermute | solution.py:28
  130.9 0.8 add_convert_fusion
  131.6 1.2 all-to-all-done.1
  132.8 0.8 shard_map.115
  (33 shorter events, 0.1 us)
Async XLA Ops:
  0.6 16.9 %collective-permute-start = (bf16[128,1024]{1,0:T(8,128)(2,1)}, bf16[128,1024]{1,0:T(8,128)(2,1)S(1)}, u32[]{:S(2)}, u32[]{:S(2)}) collective-permute-start(bf16[128,1024]{1,0:T(8,128)(2,1)} %refs_3_.3), channel_id=1, source_target_pairs={{0,4},{4,0},{8,12},{12,8},{16,20},{20,16},{24,28},{28,24},{32,36},... | collective-permute-start | bytes 786440 | tf_op jit(solution)/shard_map/ppermute | solution.py:18
  2.6 14.9 %collective-permute-start.1 = (bf16[128,1024]{1,0:T(8,128)(2,1)}, bf16[128,1024]{1,0:T(8,128)(2,1)S(1)}, u32[]{:S(2)}, u32[]{:S(2)}) collective-permute-start(bf16[128,1024]{1,0:T(8,128)(2,1)} %refs_3_.3), channel_id=1, source_target_pairs={{0,252},{4,8},{8,4},{12,16},{16,12},{20,24},{24,20},{28,32},{32,28... | collective-permute-start | bytes 786440 | tf_op jit(solution)/shard_map/ppermute | solution.py:18
  9.7 1.9 %copy-start = (bf16[4,6,256,256]{3,2,1,0:T(8,128)(2,1)S(1)}, bf16[4,6,256,256]{3,2,1,0:T(8,128)(2,1)}, u32[]{:S(2)}) copy-start(bf16[4,6,256,256]{3,2,1,0:T(8,128)(2,1)} %refs_8_.3) | copy-start | bytes 9437188
  11.6 0.9 copy-start.3
  12.5 0.7 copy-start.6
  13.2 0.7 copy-start.8
  13.9 0.7 copy-start.10
  14.5 31.8 %copy-start.1 = (bf16[4,6,256,256]{3,2,1,0:T(8,128)(2,1)S(1)}, bf16[4,6,256,256]{3,2,1,0:T(8,128)(2,1)}, u32[]{:S(2)}) copy-start(bf16[4,6,256,256]{3,2,1,0:T(8,128)(2,1)} %refs_8_.3) | copy-start | bytes 9437188
  14.5 31.8 %copy-start.4 = (bf16[128,1024]{1,0:T(8,128)(2,1)S(1)}, bf16[128,1024]{1,0:T(8,128)(2,1)}, u32[]{:S(2)}) copy-start(bf16[128,1024]{1,0:T(8,128)(2,1)} %refs_3_.3) | copy-start | bytes 786436
  14.5 31.8 %copy-start.5 = (bf16[128,512]{1,0:T(8,128)(2,1)S(1)}, bf16[128,512]{1,0:T(8,128)(2,1)}, u32[]{:S(2)}) copy-start(bf16[128,512]{1,0:T(8,128)(2,1)} %refs_9_.2) | copy-start | bytes 393220
  14.5 31.8 %copy-start.7 = (s32[4,6]{1,0:T(4,128)S(1)}, s32[4,6]{1,0:T(4,128)}, u32[]{:S(2)}) copy-start(s32[4,6]{1,0:T(4,128)} %refs_0_.5) | copy-start | bytes 292
  14.5 31.9 %copy-start.9 = (s32[256]{0:T(256)S(1)}, s32[256]{0:T(256)}, u32[]{:S(2)}) copy-start(s32[256]{0:T(256)} %refs_2_.5) | copy-start | bytes 3076
  14.5 31.9 %copy-start.11 = (s32[4]{0:T(128)S(1)}, s32[4]{0:T(128)}, u32[]{:S(2)}) copy-start(s32[4]{0:T(128)} %refs_1_.5) | copy-start | bytes 52
  17.6 13.2 %collective-permute-start.2 = (bf16[256,1024]{1,0:T(8,128)(2,1)S(1)}, bf16[256,1024]{1,0:T(8,128)(2,1)S(1)}, u32[]{:S(2)}, u32[]{:S(2)}) collective-permute-start(bf16[256,1024]{1,0:T(8,128)(2,1)S(1)} %get-tuple-element.32), channel_id=1, source_target_pairs={{0,4},{4,0},{8,12},{12,8},{16,20},{20,16},{24,28},{28,24},{32,36},... | collective-permute-start | bytes 1572872 | tf_op jit(solution)/shard_map/ppermute | solution.py:18
  17.7 17.4 %collective-permute-start.3 = (bf16[256,1024]{1,0:T(8,128)(2,1)S(1)}, bf16[256,1024]{1,0:T(8,128)(2,1)S(1)}, u32[]{:S(2)}, u32[]{:S(2)}) collective-permute-start(bf16[256,1024]{1,0:T(8,128)(2,1)S(1)} %get-tuple-element.33), channel_id=1, source_target_pairs={{0,252},{4,8},{8,4},{12,16},{16,12},{20,24},{24,20},{28,32},{32,28... | collective-permute-start | bytes 1572872 | tf_op jit(solution)/shard_map/ppermute | solution.py:18
  35.3 6.6 %collective-permute-start.4 = (bf16[128,1024]{1,0:T(8,128)(2,1)S(1)}, bf16[128,1024]{1,0:T(8,128)(2,1)S(1)}, u32[]{:S(2)}, u32[]{:S(2)}) collective-permute-start(bf16[128,1024]{1,0:T(8,128)(2,1)S(1)} %get-tuple-element.34), channel_id=1, source_target_pairs={{0,4},{4,0},{8,12},{12,8},{16,20},{20,16},{24,28},{28,24},{32,36},... | collective-permute-start | bytes 786440 | tf_op jit(solution)/shard_map/ppermute | solution.py:18
  35.4 10.9 %collective-permute-start.5 = (bf16[128,1024]{1,0:T(8,128)(2,1)S(1)}, bf16[128,1024]{1,0:T(8,128)(2,1)S(1)}, u32[]{:S(2)}, u32[]{:S(2)}) collective-permute-start(bf16[128,1024]{1,0:T(8,128)(2,1)S(1)} %get-tuple-element.35), channel_id=1, source_target_pairs={{0,252},{4,8},{8,4},{12,16},{16,12},{20,24},{24,20},{28,32},{32,28... | collective-permute-start | bytes 786440 | tf_op jit(solution)/shard_map/ppermute | solution.py:18
  46.4 19.2 %copy-start.2 = (bf16[128,512]{1,0:T(8,128)(2,1)S(1)}, bf16[128,512]{1,0:T(8,128)(2,1)}, u32[]{:S(2)}) copy-start(bf16[128,512]{1,0:T(8,128)(2,1)} %weight.1) | copy-start | bytes 393220
  49.4 2.8 %collective-permute-start.6 = (bf16[256,1024]{1,0:T(8,128)(2,1)S(1)}, bf16[256,1024]{1,0:T(8,128)(2,1)S(1)}, u32[]{:S(2)}, u32[]{:S(2)}) collective-permute-start(bf16[256,1024]{1,0:T(8,128)(2,1)S(1)} %get-tuple-element.37), channel_id=1, source_target_pairs={{0,1},{1,0},{2,3},{3,2},{4,5},{5,4},{6,7},{7,6},{8,9},{9,8},{10,11... | collective-permute-start | bytes 1572872 | tf_op jit(solution)/shard_map/ppermute | solution.py:28
  49.5 10.7 %collective-permute-start.14 = (bf16[128,1024]{1,0:T(8,128)(2,1)S(1)}, bf16[128,1024]{1,0:T(8,128)(2,1)S(1)}, u32[]{:S(2)}, u32[]{:S(2)}) collective-permute-start(bf16[128,1024]{1,0:T(8,128)(2,1)S(1)} %shard_map.106._.refs_0_), channel_id=1, source_target_pairs={{0,2},{1,3},{2,0},{3,1},{4,6},{5,7},{6,4},{7,5},{8,10},{9,11},{10,... | collective-permute-start | bytes 786440 | tf_op jit(solution)/shard_map/ppermute | solution.py:28
  52.3 13.0 %collective-permute-start.7 = (bf16[128,1024]{1,0:T(8,128)(2,1)S(1)}, bf16[128,1024]{1,0:T(8,128)(2,1)S(1)}, u32[]{:S(2)}, u32[]{:S(2)}) collective-permute-start(bf16[128,1024]{1,0:T(8,128)(2,1)S(1)} %get-tuple-element.39), channel_id=1, source_target_pairs={{0,2},{1,3},{2,0},{3,1},{4,6},{5,7},{6,4},{7,5},{8,10},{9,11},{10,... | collective-permute-start | bytes 786440 | tf_op jit(solution)/shard_map/ppermute | solution.py:28
  54.2 11.4 %collective-permute-start.15 = (bf16[128,1024]{1,0:T(8,128)(2,1)S(1)}, bf16[128,1024]{1,0:T(8,128)(2,1)S(1)}, u32[]{:S(2)}, u32[]{:S(2)}) collective-permute-start(bf16[128,1024]{1,0:T(8,128)(2,1)S(1)} %shard_map.106._.refs_0_), channel_id=1, source_target_pairs={{0,1},{1,0},{2,3},{3,2},{4,5},{5,4},{6,7},{7,6},{8,9},{9,8},{10,11... | collective-permute-start | bytes 786440 | tf_op jit(solution)/shard_map/ppermute | solution.py:28
  60.2 5.4 %collective-permute-start.16 = (bf16[128,1024]{1,0:T(8,128)(2,1)S(1)}, bf16[128,1024]{1,0:T(8,128)(2,1)S(1)}, u32[]{:S(2)}, u32[]{:S(2)}) collective-permute-start(bf16[128,1024]{1,0:T(8,128)(2,1)S(1)} %collective-permute-done.14.refs_1_), channel_id=1, source_target_pairs={{0,1},{1,0},{2,3},{3,2},{4,5},{5,4},{6,7},{7,6},{8,9},{9,8},{10,11... | collective-permute-start | bytes 786440 | tf_op jit(solution)/shard_map/ppermute | solution.py:28
  66.3 9.5 %collective-permute-start.17 = (bf16[128,1024]{1,0:T(8,128)(2,1)S(1)}, bf16[128,1024]{1,0:T(8,128)(2,1)S(1)}, u32[]{:S(2)}, u32[]{:S(2)}) collective-permute-start(bf16[128,1024]{1,0:T(8,128)(2,1)S(1)} %get-tuple-element.48.refs_0_), channel_id=1, source_target_pairs={{0,2},{1,3},{2,0},{3,1},{4,6},{5,7},{6,4},{7,5},{8,10},{9,11},{10,... | collective-permute-start | bytes 786440 | tf_op jit(solution)/shard_map/ppermute | solution.py:28
  69.0 16.7 %collective-permute-start.11 = (bf16[128,1024]{1,0:T(8,128)(2,1)S(1)}, bf16[128,1024]{1,0:T(8,128)(2,1)S(1)}, u32[]{:S(2)}, u32[]{:S(2)}) collective-permute-start(bf16[128,1024]{1,0:T(8,128)(2,1)S(1)} %get-tuple-element.40.refs_3_.hidden), channel_id=1, source_target_pairs={{0,248},{4,252},{8,16},{12,20},{16,8},{20,12},{24,32},{28,36},{32,... | collective-permute-start | bytes 786440 | tf_op jit(solution)/shard_map/ppermute | solution.py:18
  69.2 16.5 %collective-permute-start.10 = (bf16[128,1024]{1,0:T(8,128)(2,1)S(1)}, bf16[128,1024]{1,0:T(8,128)(2,1)S(1)}, u32[]{:S(2)}, u32[]{:S(2)}) collective-permute-start(bf16[128,1024]{1,0:T(8,128)(2,1)S(1)} %get-tuple-element.40.refs_3_.hidden), channel_id=1, source_target_pairs={{0,8},{4,12},{8,0},{12,4},{16,24},{20,28},{24,16},{28,20},{32,40},... | collective-permute-start | bytes 786440 | tf_op jit(solution)/shard_map/ppermute | solution.py:18
  69.2 19.9 %collective-permute-start.9 = (bf16[128,1024]{1,0:T(8,128)(2,1)S(1)}, bf16[128,1024]{1,0:T(8,128)(2,1)S(1)}, u32[]{:S(2)}, u32[]{:S(2)}) collective-permute-start(bf16[128,1024]{1,0:T(8,128)(2,1)S(1)} %get-tuple-element.40.refs_3_.hidden), channel_id=1, source_target_pairs={{0,252},{4,8},{8,4},{12,16},{16,12},{20,24},{24,20},{28,32},{32,28... | collective-permute-start | bytes 786440 | tf_op jit(solution)/shard_map/ppermute | solution.py:18
  72.0 17.1 %collective-permute-start.8 = (bf16[128,1024]{1,0:T(8,128)(2,1)S(1)}, bf16[128,1024]{1,0:T(8,128)(2,1)S(1)}, u32[]{:S(2)}, u32[]{:S(2)}) collective-permute-start(bf16[128,1024]{1,0:T(8,128)(2,1)S(1)} %get-tuple-element.40.refs_3_.hidden), channel_id=1, source_target_pairs={{0,4},{4,0},{8,12},{12,8},{16,20},{20,16},{24,28},{28,24},{32,36},... | collective-permute-start | bytes 786440 | tf_op jit(solution)/shard_map/ppermute | solution.py:18
  75.8 16.4 %collective-permute-start.18 = (bf16[128,1024]{1,0:T(8,128)(2,1)S(1)}, bf16[128,1024]{1,0:T(8,128)(2,1)S(1)}, u32[]{:S(2)}, u32[]{:S(2)}) collective-permute-start(bf16[128,1024]{1,0:T(8,128)(2,1)S(1)} %get-tuple-element.48.refs_0_), channel_id=1, source_target_pairs={{0,1},{1,0},{2,3},{3,2},{4,5},{5,4},{6,7},{7,6},{8,9},{9,8},{10,11... | collective-permute-start | bytes 786440 | tf_op jit(solution)/shard_map/ppermute | solution.py:28
  85.6 6.6 %collective-permute-start.19 = (bf16[128,1024]{1,0:T(8,128)(2,1)S(1)}, bf16[128,1024]{1,0:T(8,128)(2,1)S(1)}, u32[]{:S(2)}, u32[]{:S(2)}) collective-permute-start(bf16[128,1024]{1,0:T(8,128)(2,1)S(1)} %collective-permute-done.17.refs_1_), channel_id=1, source_target_pairs={{0,1},{1,0},{2,3},{3,2},{4,5},{5,4},{6,7},{7,6},{8,9},{9,8},{10,11... | collective-permute-start | bytes 786440 | tf_op jit(solution)/shard_map/ppermute | solution.py:28
  92.1 28.0 %collective-permute-start.12 = (bf16[256,1024]{1,0:T(8,128)(2,1)S(1)}, bf16[256,1024]{1,0:T(8,128)(2,1)S(1)}, u32[]{:S(2)}, u32[]{:S(2)}) collective-permute-start(bf16[256,1024]{1,0:T(8,128)(2,1)S(1)} %get-tuple-element.42), channel_id=1, source_target_pairs={{0,1},{1,0},{2,3},{3,2},{4,5},{5,4},{6,7},{7,6},{8,9},{9,8},{10,11... | collective-permute-start | bytes 1572872 | tf_op jit(solution)/shard_map/ppermute | solution.py:28
  115.2 17.6 %all-to-all-start.1 = ((bf16[64,16,128]{2,1,0:T(8,128)(2,1)}), bf16[64,16,128]{2,1,0:T(8,128)(2,1)S(1)}, u32[]{:S(2)}, u32[]{:S(2)}) async-start(bf16[64,16,128]{2,1,0:T(8,128)(2,1)} %bitcast.2), calls=%async_computation.1 | async-start | bytes 524288 | tf_op jit(solution)/shard_map/all_to_all | solution.py:327
  120.2 10.6 %collective-permute-start.13 = (bf16[128,1024]{1,0:T(8,128)(2,1)S(1)}, bf16[128,1024]{1,0:T(8,128)(2,1)S(1)}, u32[]{:S(2)}, u32[]{:S(2)}) collective-permute-start(bf16[128,1024]{1,0:T(8,128)(2,1)S(1)} %get-tuple-element.44), channel_id=1, source_target_pairs={{0,2},{1,3},{2,0},{3,1},{4,6},{5,7},{6,4},{7,5},{8,10},{9,11},{10,... | collective-permute-start | bytes 786440 | tf_op jit(solution)/shard_map/ppermute | solution.py:28

commit v4 on v3

--- a/solution.py
+++ b/solution.py
@@ -292,10 +292,9 @@
     ]
     spread = call(add_kernel, node, [VMEM] * 3, parts[0], *came_parts)
     ax_rows, keep, send = call(
-        lambda _, *refs: first_kernel(peers, *refs),
+        lambda *refs: first_kernel(peers, *refs),
         (node, half, half),
-        [ANY] + [SMEM] * 3 + [VMEM] * 7,
-        spread,
+        [SMEM] * 3 + [VMEM] * 7,
         *lists,
         node_features,
         *near,

time: 134 us -> 134 us (level)
  waiting for transfers between devices: 58.6 us -> 61.8 us
  starting transfers between devices: 34.3 us -> 31.5 us
    ppermute x10, waiting for transfers between devices: 33.5 us -> 36.8 us  [swap(): lax.ppermute(array, 'blk', [(i, ((i + shift ^ step) - shift) % peers) for...]
    ppermute x10, starting transfers between devices: 21.9 us -> 20 us  [swap(): lax.ppermute(array, 'blk', [(i, ((i + shift ^ step) - shift) % peers) for...]
where the time goes in v4:
time: 134 us
  waiting for transfers between devices  61.8 us (46%)
  starting transfers between devices  31.5 us (24%)
  blocking collectives  20.7 us (15%)
  Pallas kernels  13.4 us (10%)
  local copies, waits for them, and re-layouts  4.88 us (4%)
    ppermute x10, waiting for transfers between devices, swap(): lax.ppermute(array, 'blk', [(i, ((i + shift ^ step) - shift) % peers) for...  36.8 us
    ppermute x10, waiting for transfers between devices, across(): lax.ppermute(array, 'rep', [(i, i ^ flip) for i in range(lax.axis_size('r...  23.9 us
    all_to_all x1, blocking collectives, body(): got = lax.all_to_all(terms, 'blk', 0, 0, tiled=True)  20.7 us
    ppermute x10, starting transfers between devices, swap(): lax.ppermute(array, 'blk', [(i, ((i + shift ^ step) - shift) % peers) for...  20 us
    pallas_call x13, Pallas kernels, call(): pl.pallas_call(kernel, out_shape=outs, in_specs=in_specs, out_specs=out_s...  13.4 us
    ppermute x10, starting transfers between devices, across(): lax.ppermute(array, 'rep', [(i, i ^ flip) for i in range(lax.axis_size('r...  6.67 us
    unnamed x24, local copies, waits for them, and re-layouts  4.88 us
    all_to_all x1, starting transfers between devices, body(): everyone = lax.all_to_all(chunks, 'blk', 0, 0, tiled=True)  4.88 us
  transfers between devices with their start and end apart: 21, of which 11 were waited for; matrix products, arithmetic and copies ran while one was open for 1% of the time, Pallas kernels for 6%

profile of v4, /device:TPU:8, one launch (start us, length us, event | category | flops | bytes accessed | tf_op | source)
XLA Modules:
  0.0 134.0 jit_solution(17837850325975235863)
XLA Ops:
  0.6 2.0 %collective-permute-start = (bf16[128,1024]{1,0:T(8,128)(2,1)}, bf16[128,1024]{1,0:T(8,128)(2,1)S(1)}, u32[]{:S(2)}, u32[]{:S(2)}) collective-permute-start(bf16[128,1024]{1,0:T(8,128)(2,1)} %refs_3_.3), channel_id=1, source_target_pairs={{0,4},{4,0},{8,12},{12,8},{16,20},{20,16},{24,28},{28,24},{32,36},... | collective-permute-start | bytes 786440 | tf_op jit(solution)/shard_map/ppermute | solution.py:18
  2.6 7.0 %collective-permute-start.1 = (bf16[128,1024]{1,0:T(8,128)(2,1)}, bf16[128,1024]{1,0:T(8,128)(2,1)S(1)}, u32[]{:S(2)}, u32[]{:S(2)}) collective-permute-start(bf16[128,1024]{1,0:T(8,128)(2,1)} %refs_3_.3), channel_id=1, source_target_pairs={{0,252},{4,8},{8,4},{12,16},{16,12},{20,24},{24,20},{28,32},{32,28... | collective-permute-start | bytes 786440 | tf_op jit(solution)/shard_map/ppermute | solution.py:18
  9.7 1.9 %copy-done = bf16[4,6,256,256]{3,2,1,0:T(8,128)(2,1)S(1)} copy-done((bf16[4,6,256,256]{3,2,1,0:T(8,128)(2,1)S(1)}, bf16[4,6,256,256]{3,2,1,0:T(8,128)(2,1)}, u32[]{:S(2)}) %copy-start) | copy-done | bytes 3145752
  11.6 0.9 copy-done.3
  12.5 0.7 copy-done.6
  13.2 0.7 copy-done.8
  13.9 0.7 copy-done.10
  14.6 3.3 %shard_map.103 = (bf16[128,1024]{1,0:T(8,128)(2,1)S(1)}, bf16[128,1024]{1,0:T(8,128)(2,1)S(1)}, bf16[128,1024]{1,0:T(8,128)(2,1)S(1)}, bf16[128,1024]{1,0:T(8,128)(2,1)S(1)}, bf16[128,1024]{1,0:T(8,128)(2,1)S(1)}) custom-call(s32[4,6]{1,0:T(4,128)S(1)} %copy-done.6, s32[4]{0:T(128)S(1)} %copy-done.10, s32[256]{0:T(256)S(1)} %copy-done.8, ...), custom_call_target="tpu_custom_call" | custom-call | tf_op jit(solution)/shard_map/pallas_call | solution.py:254
  17.9 0.1 shard_map.104
  18.0 0.1 collective-permute-start.2
  18.1 4.1 %collective-permute-start.3 = (bf16[256,1024]{1,0:T(8,128)(2,1)S(1)}, bf16[256,1024]{1,0:T(8,128)(2,1)S(1)}, u32[]{:S(2)}, u32[]{:S(2)}) collective-permute-start(bf16[256,1024]{1,0:T(8,128)(2,1)S(1)} %get-tuple-element.30), channel_id=1, source_target_pairs={{0,252},{4,8},{8,4},{12,16},{16,12},{20,24},{24,20},{28,32},{32,28... | collective-permute-start | bytes 1572872 | tf_op jit(solution)/shard_map/ppermute | solution.py:18
  22.1 9.0 %collective-permute-done.2.refs_6_.refs_2_ = bf16[256,1024]{1,0:T(8,128)(2,1)S(1)} collective-permute-done((bf16[256,1024]{1,0:T(8,128)(2,1)S(1)}, bf16[256,1024]{1,0:T(8,128)(2,1)S(1)}, u32[]{:S(2)}, u32[]{:S(2)}) %collective-permute-start.2) | collective-permute-done | bytes 524320 | tf_op jit(solution)/shard_map/ppermute | solution.py:18
  31.1 4.3 %collective-permute-done.3.refs_7_.refs_3_ = bf16[256,1024]{1,0:T(8,128)(2,1)S(1)} collective-permute-done((bf16[256,1024]{1,0:T(8,128)(2,1)S(1)}, bf16[256,1024]{1,0:T(8,128)(2,1)S(1)}, u32[]{:S(2)}, u32[]{:S(2)}) %collective-permute-start.3) | collective-permute-done | bytes 524320 | tf_op jit(solution)/shard_map/ppermute | solution.py:18
  35.5 3.3 %shard_map.105 = (bf16[128,1024]{1,0:T(8,128)(2,1)S(1)}, bf16[256,1024]{1,0:T(8,128)(2,1)S(1)}, bf16[256,1024]{1,0:T(8,128)(2,1)S(1)}) custom-call(s32[4,6]{1,0:T(4,128)S(1)} %copy-done.7, s32[4]{0:T(128)S(1)} %copy-done.11, s32[256]{0:T(256)S(1)} %copy-done.9, bf16[128,1024]{1,0:T(8,128)(2,1)S(1)} %copy-done.4, ...), custom_call_target="tpu_custom_call" | custom-call | tf_op jit(solution)/shard_map/pallas_call | solution.py:254
  38.8 0.0 copy-start.2
  38.8 0.1 collective-permute-start.4
  38.9 0.1 shard_map.110
  39.1 0.1 collective-permute-start.12
  39.2 2.3 %collective-permute-start.13 = (bf16[128,1024]{1,0:T(8,128)(2,1)S(1)}, bf16[128,1024]{1,0:T(8,128)(2,1)S(1)}, u32[]{:S(2)}, u32[]{:S(2)}) collective-permute-start(bf16[128,1024]{1,0:T(8,128)(2,1)S(1)} %get-tuple-element.46), channel_id=1, source_target_pairs={{0,252},{4,8},{8,4},{12,16},{16,12},{20,24},{24,20},{28,32},{32,28... | collective-permute-start | bytes 786440 | tf_op jit(solution)/shard_map/ppermute | solution.py:18
  41.5 6.3 %collective-permute-done.12.came_ahead = bf16[128,1024]{1,0:T(8,128)(2,1)S(1)} collective-permute-done((bf16[128,1024]{1,0:T(8,128)(2,1)S(1)}, bf16[128,1024]{1,0:T(8,128)(2,1)S(1)}, u32[]{:S(2)}, u32[]{:S(2)}) %collective-permute-start.12) | collective-permute-done | bytes 262176 | tf_op jit(solution)/shard_map/ppermute | solution.py:18
  47.8 4.3 %collective-permute-done.13.came_back = bf16[128,1024]{1,0:T(8,128)(2,1)S(1)} collective-permute-done((bf16[128,1024]{1,0:T(8,128)(2,1)S(1)}, bf16[128,1024]{1,0:T(8,128)(2,1)S(1)}, u32[]{:S(2)}, u32[]{:S(2)}) %collective-permute-start.13) | collective-permute-done | bytes 262176 | tf_op jit(solution)/shard_map/ppermute | solution.py:18
  52.2 0.1 shard_map.111.refs_0_
  52.3 2.7 %collective-permute-start.14 = (bf16[128,1024]{1,0:T(8,128)(2,1)S(1)}, bf16[128,1024]{1,0:T(8,128)(2,1)S(1)}, u32[]{:S(2)}, u32[]{:S(2)}) collective-permute-start(bf16[128,1024]{1,0:T(8,128)(2,1)S(1)} %shard_map.111.refs_0_), channel_id=1, source_target_pairs={{0,2},{1,3},{2,0},{3,1},{4,6},{5,7},{6,4},{7,5},{8,10},{9,11},{10,... | collective-permute-start | bytes 786440 | tf_op jit(solution)/shard_map/ppermute | solution.py:28
  55.0 0.1 shard_map.106
  55.1 1.0 collective-permute-start.5
  56.1 7.0 %collective-permute-done.14.refs_1_ = bf16[128,1024]{1,0:T(8,128)(2,1)S(1)} collective-permute-done((bf16[128,1024]{1,0:T(8,128)(2,1)S(1)}, bf16[128,1024]{1,0:T(8,128)(2,1)S(1)}, u32[]{:S(2)}, u32[]{:S(2)}) %collective-permute-start.14) | collective-permute-done | bytes 262176 | tf_op jit(solution)/shard_map/ppermute | solution.py:28
  63.1 4.3 %collective-permute-done.5.came = bf16[128,1024]{1,0:T(8,128)(2,1)S(1)} collective-permute-done((bf16[128,1024]{1,0:T(8,128)(2,1)S(1)}, bf16[128,1024]{1,0:T(8,128)(2,1)S(1)}, u32[]{:S(2)}, u32[]{:S(2)}) %collective-permute-start.5) | collective-permute-done | bytes 262176 | tf_op jit(solution)/shard_map/ppermute | solution.py:28
  67.4 0.2 shard_map.107
  67.7 0.7 shard_map.112
  68.4 2.7 %collective-permute-start.17 = (bf16[128,1024]{1,0:T(8,128)(2,1)S(1)}, bf16[128,1024]{1,0:T(8,128)(2,1)S(1)}, u32[]{:S(2)}, u32[]{:S(2)}) collective-permute-start(bf16[128,1024]{1,0:T(8,128)(2,1)S(1)} %get-tuple-element.48.refs_0_), channel_id=1, source_target_pairs={{0,2},{1,3},{2,0},{3,1},{4,6},{5,7},{6,4},{7,5},{8,10},{9,11},{10,... | collective-permute-start | bytes 786440 | tf_op jit(solution)/shard_map/ppermute | solution.py:28
  71.0 0.0 collective-permute-start.8
  71.1 2.9 %collective-permute-start.7 = (bf16[128,1024]{1,0:T(8,128)(2,1)S(1)}, bf16[128,1024]{1,0:T(8,128)(2,1)S(1)}, u32[]{:S(2)}, u32[]{:S(2)}) collective-permute-start(bf16[128,1024]{1,0:T(8,128)(2,1)S(1)} %get-tuple-element.35.refs_3_.hidden), channel_id=1, source_target_pairs={{0,252},{4,8},{8,4},{12,16},{16,12},{20,24},{24,20},{28,32},{32,28... | collective-permute-start | bytes 786440 | tf_op jit(solution)/shard_map/ppermute | solution.py:18
  73.9 1.5 %collective-permute-start.6 = (bf16[128,1024]{1,0:T(8,128)(2,1)S(1)}, bf16[128,1024]{1,0:T(8,128)(2,1)S(1)}, u32[]{:S(2)}, u32[]{:S(2)}) collective-permute-start(bf16[128,1024]{1,0:T(8,128)(2,1)S(1)} %get-tuple-element.35.refs_3_.hidden), channel_id=1, source_target_pairs={{0,4},{4,0},{8,12},{12,8},{16,20},{20,16},{24,28},{28,24},{32,36},... | collective-permute-start | bytes 786440 | tf_op jit(solution)/shard_map/ppermute | solution.py:18
  75.4 2.0 %collective-permute-done.17.refs_1_ = bf16[128,1024]{1,0:T(8,128)(2,1)S(1)} collective-permute-done((bf16[128,1024]{1,0:T(8,128)(2,1)S(1)}, bf16[128,1024]{1,0:T(8,128)(2,1)S(1)}, u32[]{:S(2)}, u32[]{:S(2)}) %collective-permute-start.17) | collective-permute-done | bytes 262176 | tf_op jit(solution)/shard_map/ppermute | solution.py:28
  77.4 9.8 %collective-permute-done.9.refs_7_ = bf16[128,1024]{1,0:T(8,128)(2,1)S(1)} collective-permute-done((bf16[128,1024]{1,0:T(8,128)(2,1)S(1)}, bf16[128,1024]{1,0:T(8,128)(2,1)S(1)}, u32[]{:S(2)}, u32[]{:S(2)}) %collective-permute-start.9) | collective-permute-done | bytes 262176 | tf_op jit(solution)/shard_map/ppermute | solution.py:18
  87.2 3.0 %collective-permute-done.7.refs_5_ = bf16[128,1024]{1,0:T(8,128)(2,1)S(1)} collective-permute-done((bf16[128,1024]{1,0:T(8,128)(2,1)S(1)}, bf16[128,1024]{1,0:T(8,128)(2,1)S(1)}, u32[]{:S(2)}, u32[]{:S(2)}) %collective-permute-start.7) | collective-permute-done | bytes 262176 | tf_op jit(solution)/shard_map/ppermute | solution.py:18
  90.2 3.3 %shard_map.108 = (bf16[256,1024]{1,0:T(8,128)(2,1)S(1)}, bf16[256,1024]{1,0:T(8,128)(2,1)S(1)}) custom-call(s32[4,6]{1,0:T(4,128)S(1)} %copy-done.7, s32[4]{0:T(128)S(1)} %copy-done.11, s32[256]{0:T(256)S(1)} %copy-done.9, bf16[128,1024]{1,0:T(8,128)(2,1)S(1)} %get-tuple-element.35.refs_3_.hidden, bf16[128,1024]{1,0:T(8,128)(2,1)S(1)} %collective-permute-done.6.refs_4_, ...), custom_call_target="tpu_custom_call" | custom-call | tf_op jit(solution)/shard_map/pallas_call | solution.py:254
  93.5 0.1 collective-permute-start.10
  93.6 0.4 shard_map.113
  94.1 20.7 %all_to_all.22 = bf16[64,16,128]{2,1,0:T(8,128)(2,1)S(1)} all-to-all(bf16[64,16,128]{2,1,0:T(8,128)(2,1)S(1)} %bitcast.6), channel_id=1, replica_groups=mesh['blk'=64,'rep'=4] {'blk'}, dimensions={0} | all-to-all | bytes 524288 | tf_op jit(solution)/shard_map/all_to_all | solution.py:324
  114.7 0.8 shard_map.114
  115.5 4.9 %all-to-all-start.1 = ((bf16[64,16,128]{2,1,0:T(8,128)(2,1)}), bf16[64,16,128]{2,1,0:T(8,128)(2,1)S(1)}, u32[]{:S(2)}, u32[]{:S(2)}) async-start(bf16[64,16,128]{2,1,0:T(8,128)(2,1)} %bitcast.2), calls=%async_computation.1 | async-start | bytes 524288 | tf_op jit(solution)/shard_map/all_to_all | solution.py:326
  120.4 0.1 shard_map.109
  120.6 0.1 collective-permute-start.11
  120.7 10.5 %collective-permute-done.11 = bf16[128,1024]{1,0:T(8,128)(2,1)S(1)} collective-permute-done((bf16[128,1024]{1,0:T(8,128)(2,1)S(1)}, bf16[128,1024]{1,0:T(8,128)(2,1)S(1)}, u32[]{:S(2)}, u32[]{:S(2)}) %collective-permute-start.11) | collective-permute-done | bytes 262176 | tf_op jit(solution)/shard_map/ppermute | solution.py:28
  131.2 0.8 add_convert_fusion
  131.9 1.2 all-to-all-done.1
  133.1 0.8 shard_map.115
  (33 shorter events, 0.1 us)
Async XLA Ops:
  0.6 17.2 %collective-permute-start = (bf16[128,1024]{1,0:T(8,128)(2,1)}, bf16[128,1024]{1,0:T(8,128)(2,1)S(1)}, u32[]{:S(2)}, u32[]{:S(2)}) collective-permute-start(bf16[128,1024]{1,0:T(8,128)(2,1)} %refs_3_.3), channel_id=1, source_target_pairs={{0,4},{4,0},{8,12},{12,8},{16,20},{20,16},{24,28},{28,24},{32,36},... | collective-permute-start | bytes 786440 | tf_op jit(solution)/shard_map/ppermute | solution.py:18
  2.6 15.2 %collective-permute-start.1 = (bf16[128,1024]{1,0:T(8,128)(2,1)}, bf16[128,1024]{1,0:T(8,128)(2,1)S(1)}, u32[]{:S(2)}, u32[]{:S(2)}) collective-permute-start(bf16[128,1024]{1,0:T(8,128)(2,1)} %refs_3_.3), channel_id=1, source_target_pairs={{0,252},{4,8},{8,4},{12,16},{16,12},{20,24},{24,20},{28,32},{32,28... | collective-permute-start | bytes 786440 | tf_op jit(solution)/shard_map/ppermute | solution.py:18
  9.7 1.9 %copy-start = (bf16[4,6,256,256]{3,2,1,0:T(8,128)(2,1)S(1)}, bf16[4,6,256,256]{3,2,1,0:T(8,128)(2,1)}, u32[]{:S(2)}) copy-start(bf16[4,6,256,256]{3,2,1,0:T(8,128)(2,1)} %refs_8_.3) | copy-start | bytes 9437188
  11.6 0.9 copy-start.3
  12.5 0.7 copy-start.6
  13.2 0.7 copy-start.8
  13.9 0.7 copy-start.10
  14.5 20.9 %copy-start.1 = (bf16[4,6,256,256]{3,2,1,0:T(8,128)(2,1)S(1)}, bf16[4,6,256,256]{3,2,1,0:T(8,128)(2,1)}, u32[]{:S(2)}) copy-start(bf16[4,6,256,256]{3,2,1,0:T(8,128)(2,1)} %refs_8_.3) | copy-start | bytes 9437188
  14.5 20.9 %copy-start.4 = (bf16[128,1024]{1,0:T(8,128)(2,1)S(1)}, bf16[128,1024]{1,0:T(8,128)(2,1)}, u32[]{:S(2)}) copy-start(bf16[128,1024]{1,0:T(8,128)(2,1)} %refs_3_.3) | copy-start | bytes 786436
  14.5 20.9 %copy-start.5 = (bf16[128,512]{1,0:T(8,128)(2,1)S(1)}, bf16[128,512]{1,0:T(8,128)(2,1)}, u32[]{:S(2)}) copy-start(bf16[128,512]{1,0:T(8,128)(2,1)} %refs_9_.2) | copy-start | bytes 393220
  14.5 20.9 %copy-start.7 = (s32[4,6]{1,0:T(4,128)S(1)}, s32[4,6]{1,0:T(4,128)}, u32[]{:S(2)}) copy-start(s32[4,6]{1,0:T(4,128)} %refs_0_.5) | copy-start | bytes 292
  14.5 21.0 %copy-start.9 = (s32[256]{0:T(256)S(1)}, s32[256]{0:T(256)}, u32[]{:S(2)}) copy-start(s32[256]{0:T(256)} %refs_2_.5) | copy-start | bytes 3076
  14.5 21.0 %copy-start.11 = (s32[4]{0:T(128)S(1)}, s32[4]{0:T(128)}, u32[]{:S(2)}) copy-start(s32[4]{0:T(128)} %refs_1_.5) | copy-start | bytes 52
  18.0 13.2 %collective-permute-start.2 = (bf16[256,1024]{1,0:T(8,128)(2,1)S(1)}, bf16[256,1024]{1,0:T(8,128)(2,1)S(1)}, u32[]{:S(2)}, u32[]{:S(2)}) collective-permute-start(bf16[256,1024]{1,0:T(8,128)(2,1)S(1)} %get-tuple-element.29), channel_id=1, source_target_pairs={{0,4},{4,0},{8,12},{12,8},{16,20},{20,16},{24,28},{28,24},{32,36},... | collective-permute-start | bytes 1572872 | tf_op jit(solution)/shard_map/ppermute | solution.py:18
  18.1 17.4 %collective-permute-start.3 = (bf16[256,1024]{1,0:T(8,128)(2,1)S(1)}, bf16[256,1024]{1,0:T(8,128)(2,1)S(1)}, u32[]{:S(2)}, u32[]{:S(2)}) collective-permute-start(bf16[256,1024]{1,0:T(8,128)(2,1)S(1)} %get-tuple-element.30), channel_id=1, source_target_pairs={{0,252},{4,8},{8,4},{12,16},{16,12},{20,24},{24,20},{28,32},{32,28... | collective-permute-start | bytes 1572872 | tf_op jit(solution)/shard_map/ppermute | solution.py:18
  38.8 28.8 %copy-start.2 = (bf16[128,512]{1,0:T(8,128)(2,1)S(1)}, bf16[128,512]{1,0:T(8,128)(2,1)}, u32[]{:S(2)}) copy-start(bf16[128,512]{1,0:T(8,128)(2,1)} %weight.1) | copy-start | bytes 393220
  38.8 16.1 %collective-permute-start.4 = (bf16[256,1024]{1,0:T(8,128)(2,1)S(1)}, bf16[256,1024]{1,0:T(8,128)(2,1)S(1)}, u32[]{:S(2)}, u32[]{:S(2)}) collective-permute-start(bf16[256,1024]{1,0:T(8,128)(2,1)S(1)} %get-tuple-element.32), channel_id=1, source_target_pairs={{0,1},{1,0},{2,3},{3,2},{4,5},{5,4},{6,7},{7,6},{8,9},{9,8},{10,11... | collective-permute-start | bytes 1572872 | tf_op jit(solution)/shard_map/ppermute | solution.py:28
  39.1 8.8 %collective-permute-start.12 = (bf16[128,1024]{1,0:T(8,128)(2,1)S(1)}, bf16[128,1024]{1,0:T(8,128)(2,1)S(1)}, u32[]{:S(2)}, u32[]{:S(2)}) collective-permute-start(bf16[128,1024]{1,0:T(8,128)(2,1)S(1)} %get-tuple-element.45), channel_id=1, source_target_pairs={{0,4},{4,0},{8,12},{12,8},{16,20},{20,16},{24,28},{28,24},{32,36},... | collective-permute-start | bytes 786440 | tf_op jit(solution)/shard_map/ppermute | solution.py:18
  39.2 13.0 %collective-permute-start.13 = (bf16[128,1024]{1,0:T(8,128)(2,1)S(1)}, bf16[128,1024]{1,0:T(8,128)(2,1)S(1)}, u32[]{:S(2)}, u32[]{:S(2)}) collective-permute-start(bf16[128,1024]{1,0:T(8,128)(2,1)S(1)} %get-tuple-element.46), channel_id=1, source_target_pairs={{0,252},{4,8},{8,4},{12,16},{16,12},{20,24},{24,20},{28,32},{32,28... | collective-permute-start | bytes 786440 | tf_op jit(solution)/shard_map/ppermute | solution.py:18
  52.3 10.8 %collective-permute-start.14 = (bf16[128,1024]{1,0:T(8,128)(2,1)S(1)}, bf16[128,1024]{1,0:T(8,128)(2,1)S(1)}, u32[]{:S(2)}, u32[]{:S(2)}) collective-permute-start(bf16[128,1024]{1,0:T(8,128)(2,1)S(1)} %shard_map.111.refs_0_), channel_id=1, source_target_pairs={{0,2},{1,3},{2,0},{3,1},{4,6},{5,7},{6,4},{7,5},{8,10},{9,11},{10,... | collective-permute-start | bytes 786440 | tf_op jit(solution)/shard_map/ppermute | solution.py:28
  55.1 12.3 %collective-permute-start.5 = (bf16[128,1024]{1,0:T(8,128)(2,1)S(1)}, bf16[128,1024]{1,0:T(8,128)(2,1)S(1)}, u32[]{:S(2)}, u32[]{:S(2)}) collective-permute-start(bf16[128,1024]{1,0:T(8,128)(2,1)S(1)} %get-tuple-element.34), channel_id=1, source_target_pairs={{0,2},{1,3},{2,0},{3,1},{4,6},{5,7},{6,4},{7,5},{8,10},{9,11},{10,... | collective-permute-start | bytes 786440 | tf_op jit(solution)/shard_map/ppermute | solution.py:28
  56.1 11.5 %collective-permute-start.15 = (bf16[128,1024]{1,0:T(8,128)(2,1)S(1)}, bf16[128,1024]{1,0:T(8,128)(2,1)S(1)}, u32[]{:S(2)}, u32[]{:S(2)}) collective-permute-start(bf16[128,1024]{1,0:T(8,128)(2,1)S(1)} %shard_map.111.refs_0_), channel_id=1, source_target_pairs={{0,1},{1,0},{2,3},{3,2},{4,5},{5,4},{6,7},{7,6},{8,9},{9,8},{10,11... | collective-permute-start | bytes 786440 | tf_op jit(solution)/shard_map/ppermute | solution.py:28
  63.1 4.6 %collective-permute-start.16 = (bf16[128,1024]{1,0:T(8,128)(2,1)S(1)}, bf16[128,1024]{1,0:T(8,128)(2,1)S(1)}, u32[]{:S(2)}, u32[]{:S(2)}) collective-permute-start(bf16[128,1024]{1,0:T(8,128)(2,1)S(1)} %collective-permute-done.14.refs_1_), channel_id=1, source_target_pairs={{0,1},{1,0},{2,3},{3,2},{4,5},{5,4},{6,7},{7,6},{8,9},{9,8},{10,11... | collective-permute-start | bytes 786440 | tf_op jit(solution)/shard_map/ppermute | solution.py:28
  68.4 9.0 %collective-permute-start.17 = (bf16[128,1024]{1,0:T(8,128)(2,1)S(1)}, bf16[128,1024]{1,0:T(8,128)(2,1)S(1)}, u32[]{:S(2)}, u32[]{:S(2)}) collective-permute-start(bf16[128,1024]{1,0:T(8,128)(2,1)S(1)} %get-tuple-element.48.refs_0_), channel_id=1, source_target_pairs={{0,2},{1,3},{2,0},{3,1},{4,6},{5,7},{6,4},{7,5},{8,10},{9,11},{10,... | collective-permute-start | bytes 786440 | tf_op jit(solution)/shard_map/ppermute | solution.py:28
  71.0 16.1 %collective-permute-start.9 = (bf16[128,1024]{1,0:T(8,128)(2,1)S(1)}, bf16[128,1024]{1,0:T(8,128)(2,1)S(1)}, u32[]{:S(2)}, u32[]{:S(2)}) collective-permute-start(bf16[128,1024]{1,0:T(8,128)(2,1)S(1)} %get-tuple-element.35.refs_3_.hidden), channel_id=1, source_target_pairs={{0,248},{4,252},{8,16},{12,20},{16,8},{20,12},{24,32},{28,36},{32,... | collective-permute-start | bytes 786440 | tf_op jit(solution)/shard_map/ppermute | solution.py:18
  71.0 16.2 %collective-permute-start.8 = (bf16[128,1024]{1,0:T(8,128)(2,1)S(1)}, bf16[128,1024]{1,0:T(8,128)(2,1)S(1)}, u32[]{:S(2)}, u32[]{:S(2)}) collective-permute-start(bf16[128,1024]{1,0:T(8,128)(2,1)S(1)} %get-tuple-element.35.refs_3_.hidden), channel_id=1, source_target_pairs={{0,8},{4,12},{8,0},{12,4},{16,24},{20,28},{24,16},{28,20},{32,40},... | collective-permute-start | bytes 786440 | tf_op jit(solution)/shard_map/ppermute | solution.py:18
  71.1 19.1 %collective-permute-start.7 = (bf16[128,1024]{1,0:T(8,128)(2,1)S(1)}, bf16[128,1024]{1,0:T(8,128)(2,1)S(1)}, u32[]{:S(2)}, u32[]{:S(2)}) collective-permute-start(bf16[128,1024]{1,0:T(8,128)(2,1)S(1)} %get-tuple-element.35.refs_3_.hidden), channel_id=1, source_target_pairs={{0,252},{4,8},{8,4},{12,16},{16,12},{20,24},{24,20},{28,32},{32,28... | collective-permute-start | bytes 786440 | tf_op jit(solution)/shard_map/ppermute | solution.py:18
  73.9 16.3 %collective-permute-start.6 = (bf16[128,1024]{1,0:T(8,128)(2,1)S(1)}, bf16[128,1024]{1,0:T(8,128)(2,1)S(1)}, u32[]{:S(2)}, u32[]{:S(2)}) collective-permute-start(bf16[128,1024]{1,0:T(8,128)(2,1)S(1)} %get-tuple-element.35.refs_3_.hidden), channel_id=1, source_target_pairs={{0,4},{4,0},{8,12},{12,8},{16,20},{20,16},{24,28},{28,24},{32,36},... | collective-permute-start | bytes 786440 | tf_op jit(solution)/shard_map/ppermute | solution.py:18
  77.4 16.2 %collective-permute-start.18 = (bf16[128,1024]{1,0:T(8,128)(2,1)S(1)}, bf16[128,1024]{1,0:T(8,128)(2,1)S(1)}, u32[]{:S(2)}, u32[]{:S(2)}) collective-permute-start(bf16[128,1024]{1,0:T(8,128)(2,1)S(1)} %get-tuple-element.48.refs_0_), channel_id=1, source_target_pairs={{0,1},{1,0},{2,3},{3,2},{4,5},{5,4},{6,7},{7,6},{8,9},{9,8},{10,11... | collective-permute-start | bytes 786440 | tf_op jit(solution)/shard_map/ppermute | solution.py:28
  87.2 6.4 %collective-permute-start.19 = (bf16[128,1024]{1,0:T(8,128)(2,1)S(1)}, bf16[128,1024]{1,0:T(8,128)(2,1)S(1)}, u32[]{:S(2)}, u32[]{:S(2)}) collective-permute-start(bf16[128,1024]{1,0:T(8,128)(2,1)S(1)} %collective-permute-done.17.refs_1_), channel_id=1, source_target_pairs={{0,1},{1,0},{2,3},{3,2},{4,5},{5,4},{6,7},{7,6},{8,9},{9,8},{10,11... | collective-permute-start | bytes 786440 | tf_op jit(solution)/shard_map/ppermute | solution.py:28
  93.5 26.9 %collective-permute-start.10 = (bf16[256,1024]{1,0:T(8,128)(2,1)S(1)}, bf16[256,1024]{1,0:T(8,128)(2,1)S(1)}, u32[]{:S(2)}, u32[]{:S(2)}) collective-permute-start(bf16[256,1024]{1,0:T(8,128)(2,1)S(1)} %get-tuple-element.37), channel_id=1, source_target_pairs={{0,1},{1,0},{2,3},{3,2},{4,5},{5,4},{6,7},{7,6},{8,9},{9,8},{10,11... | collective-permute-start | bytes 1572872 | tf_op jit(solution)/shard_map/ppermute | solution.py:28
  115.5 17.6 %all-to-all-start.1 = ((bf16[64,16,128]{2,1,0:T(8,128)(2,1)}), bf16[64,16,128]{2,1,0:T(8,128)(2,1)S(1)}, u32[]{:S(2)}, u32[]{:S(2)}) async-start(bf16[64,16,128]{2,1,0:T(8,128)(2,1)} %bitcast.2), calls=%async_computation.1 | async-start | bytes 524288 | tf_op jit(solution)/shard_map/all_to_all | solution.py:326
  120.6 10.6 %collective-permute-start.11 = (bf16[128,1024]{1,0:T(8,128)(2,1)S(1)}, bf16[128,1024]{1,0:T(8,128)(2,1)S(1)}, u32[]{:S(2)}, u32[]{:S(2)}) collective-permute-start(bf16[128,1024]{1,0:T(8,128)(2,1)S(1)} %get-tuple-element.39), channel_id=1, source_target_pairs={{0,2},{1,3},{2,0},{3,1},{4,6},{5,7},{6,4},{7,5},{8,10},{9,11},{10,... | collective-permute-start | bytes 786440 | tf_op jit(solution)/shard_map/ppermute | solution.py:28
